TPU v7x, 256 devices: a whole 4x4x8 slice. The times are simulated.
256 devices in a mesh: gx: 8 (over x, core), gy: 4 (over z_hi), gz: 8 (over y, z_lo).
Axes of the slice: x: 4, y: 4, z: 8 (z_hi: 4, z_lo: 2; z = z_hi * 2 + z_lo), core: 2. Of those that a mesh axis runs over, the one named last changes fastest.
Arguments:
- tokens: bfloat16 [1536, 5120], P(('gy', 'gx'), 'gz'), may hold values from -8 to 8
- gate_weight: bfloat16 [5120, 13824], P(('gz', 'gy'), 'gx'), may hold values from -0.078125 to 0.078125
- up_weight: bfloat16 [5120, 13824], P(('gz', 'gy'), 'gx'), may hold values from -0.078125 to 0.078125
- down_weight: bfloat16 [13824, 5120], P(('gx', 'gy'), 'gz'), may hold values from -0.0546875 to 0.0546875
- cotangent: bfloat16 [1536, 5120], P(('gy', 'gx'), 'gz'), may hold values from -1.5 to 1.5
- penalty_weight: float32 [5120], P('gz'), may hold values from 0.1 to 1
Outputs:
- mixed: bfloat16 [1536, 5120], P(('gy', 'gx'), 'gz')
- grad_tokens: bfloat16 [1536, 5120], P(('gy', 'gx'), 'gz')
- grad_gate: bfloat16 [5120, 13824], P(('gz', 'gy'), 'gx')
- grad_up: bfloat16 [5120, 13824], P(('gz', 'gy'), 'gx')
- grad_down: bfloat16 [13824, 5120], P(('gx', 'gy'), 'gz')
All inputs are finite; a program needn't handle non-finite values.
Results may differ from a plain program's by a relative error of at most 0.01.
Values may be sent and summed in bfloat16 or wider, within the bound.
A program may use at most 128 MiB of HBM per device.

v0:
```python
import jax
import jax.numpy as jnp
from jax import lax
from jax.sharding import PartitionSpec as P

EPSILON = 1e-05


def moment_sums(values):
    squared = values * values
    return jnp.stack(
        [
            jnp.sum(values, 0),
            jnp.sum(squared, 0),
            jnp.sum(squared * values, 0),
            jnp.sum(squared * squared, 0),
        ]
    )


def penalty_grad(values, totals, count, cotangent, weight):
    mean_value = totals[0] / count
    raw_two = totals[1] / count
    raw_three = totals[2] / count
    raw_four = totals[3] / count
    central_two = raw_two - mean_value * mean_value
    central_three = (
        raw_three - 3.0 * mean_value * raw_two + 2.0 * mean_value * mean_value * mean_value
    )
    central_four = (
        raw_four
        - 4.0 * mean_value * raw_three
        + 6.0 * mean_value * mean_value * raw_two
        - 3.0 * mean_value * mean_value * mean_value * mean_value
    )
    spread = central_two + EPSILON
    centred = values - mean_value
    extra = (centred * centred * centred - central_three) / (
        spread * spread
    ) - central_four * centred / (spread * spread * spread)
    return (cotangent.astype(jnp.float32) + weight * extra).astype(jnp.bfloat16)


def contract_rows(left, right):
    return lax.dot_general(
        left, right, (((0,), (0,)), ((), ())), preferred_element_type=jnp.float32
    )


def contract_columns(left, right):
    return lax.dot_general(
        left, right, (((1,), (1,)), ((), ())), preferred_element_type=jnp.float32
    )


def body(tokens, gate_weight, up_weight, down_weight, cotangent, penalty_weight):
    hidden_width = gate_weight.shape[1]
    own_rows = tokens.shape[0]
    count = float(own_rows * lax.axis_size("gx") * lax.axis_size("gy"))
    rows_in = lax.all_gather(tokens, "gx", axis=0, tiled=True)
    both_weights = lax.all_gather(
        jnp.concatenate([gate_weight, up_weight], 1), "gy", axis=0, tiled=True
    )
    pre_act = lax.psum_scatter(
        jnp.dot(rows_in, both_weights, preferred_element_type=jnp.float32),
        "gz",
        scatter_dimension=0,
        tiled=True,
    )
    gate = pre_act[:, :hidden_width]
    up = pre_act[:, hidden_width:]
    sigmoid_gate = jax.nn.sigmoid(gate)
    activated = gate * sigmoid_gate
    hidden = (activated * up).astype(jnp.bfloat16)
    hidden_rows = lax.all_gather(hidden, "gz", axis=0, tiled=True)
    down_full = lax.all_gather(down_weight, "gy", axis=0, tiled=True)
    result = lax.psum_scatter(
        jnp.dot(hidden_rows, down_full, preferred_element_type=jnp.float32),
        "gx",
        scatter_dimension=0,
        tiled=True,
    )
    totals = lax.psum(moment_sums(result), ("gx", "gy"))
    grad_own = penalty_grad(result, totals, count, cotangent, penalty_weight)
    grad_rows = lax.all_gather(grad_own, "gx", axis=0, tiled=True)
    mixed = result.astype(jnp.bfloat16)
    grad_hidden = lax.psum_scatter(
        contract_columns(grad_rows, down_full), "gz", scatter_dimension=0, tiled=True
    )
    grad_down = lax.psum_scatter(
        contract_rows(hidden_rows, grad_rows), "gy", scatter_dimension=0, tiled=True
    ).astype(jnp.bfloat16)
    grad_gate_act = (grad_hidden * up * sigmoid_gate * (1.0 + gate * (1.0 - sigmoid_gate))).astype(
        jnp.bfloat16
    )
    grad_up_act = (grad_hidden * activated).astype(jnp.bfloat16)
    both_grads = lax.all_gather(
        jnp.concatenate([grad_gate_act, grad_up_act], 1), "gz", axis=0, tiled=True
    )
    grad_tokens = lax.psum_scatter(
        contract_columns(both_grads, both_weights), "gx", scatter_dimension=0, tiled=True
    ).astype(jnp.bfloat16)
    weight_sums = lax.psum_scatter(
        contract_rows(rows_in, both_grads), "gy", scatter_dimension=0, tiled=True
    )
    grad_gate = weight_sums[:, :hidden_width].astype(jnp.bfloat16)
    grad_up = weight_sums[:, hidden_width:].astype(jnp.bfloat16)
    return (mixed, grad_tokens, grad_gate, grad_up, grad_down)


def solution(mesh):
    in_specs = (
        P(("gy", "gx"), "gz"),
        P(("gz", "gy"), "gx"),
        P(("gz", "gy"), "gx"),
        P(("gx", "gy"), "gz"),
        P(("gy", "gx"), "gz"),
        P("gz"),
    )
    out_specs = (
        P(("gy", "gx"), "gz"),
        P(("gy", "gx"), "gz"),
        P(("gz", "gy"), "gx"),
        P(("gz", "gy"), "gx"),
        P(("gx", "gy"), "gz"),
    )
    return jax.shard_map(body, mesh=mesh, in_specs=in_specs, out_specs=out_specs, check_vma=False)
```

profile of v0, /device:TPU:1, one launch (start us, length us, event | category | flops | bytes accessed | tf_op | source)
XLA Modules:
  0.0 959.4 jit_solution(14005765176121829149)
XLA Ops:
  7.2 2.5 pad_maximum_fusion
  9.8 16.2 %all_gather.19 = bf16[384,640]{1,0:T(8,128)(2,1)S(1)} all-gather(bf16[48,640]{1,0:T(8,128)(2,1)S(1)} %copy-done.3), channel_id=1, replica_groups=mesh['gx'=8,'gy'=4,'gz'=8] {'gx'}, dimensions={0}, use_global_device_ids=true | all-gather | bytes 552960 | tf_op jit(solution)/shard_map/all_gather | solution.py:60
  25.9 70.2 %all-gather.5.cloned.1.call-done = bf16[640,3456]{1,0:T(8,128)(2,1)} async-done(((bf16[160,3456]{1,0:T(8,128)(2,1)}), bf16[640,3456]{1,0:T(8,128)(2,1)}) %all-gather.5.cloned.1.call-update) | async-done | bytes 4423696 | tf_op jit(solution)/shard_map/all_gather | solution.py:61
  96.1 7.4 convolution_bitcast_fusion.1
  103.5 6.1 copy.28
  110.4 119.6 %reduce-scatter.19.cloned.1.call-done = f32[48,3456]{1,0:T(8,128)} async-done(((f32[384,3456]{1,0:T(8,128)}), f32[48,3456]{1,0:T(8,128)}) %reduce-scatter.19.cloned.1.call-update) | async-done | bytes 663568 | tf_op jit(solution)/shard_map/reduce_scatter | solution.py:64
  230.0 1.9 multiply_convert_fusion.2
  232.0 52.0 %all-gather.9.cloned.1.call-done = bf16[1728,640]{1,0:T(8,128)(2,1)} async-done(((bf16[432,640]{1,0:T(8,128)(2,1)}), bf16[1728,640]{1,0:T(8,128)(2,1)}) %all-gather.9.cloned.1.call-update) | async-done | bytes 2211856 | tf_op jit(solution)/shard_map/all_gather | solution.py:76
  284.1 43.2 %all-gather.7.cloned.1.call-done = bf16[384,1728]{1,0:T(8,128)(2,1)} async-done(((bf16[48,1728]{1,0:T(8,128)(2,1)}), bf16[384,1728]{1,0:T(8,128)(2,1)}) %all-gather.7.cloned.1.call-update) | async-done | bytes 1327120 | tf_op jit(solution)/shard_map/all_gather | solution.py:75
  327.3 4.2 fusion.19
  331.6 34.3 %reduce-scatter.13.cloned.1.call-done = f32[48,640]{1,0:T(8,128)} async-done(((f32[384,640]{1,0:T(8,128)}), f32[48,640]{1,0:T(8,128)}) %reduce-scatter.13.cloned.1.call-update) | async-done | bytes 122896 | tf_op jit(solution)/shard_map/reduce_scatter | solution.py:77
  365.9 1.0 fusion.17
  366.9 140.9 %psum.7 = f32[4,640]{1,0:T(4,128)S(1)} all-reduce(f32[4,640]{1,0:T(4,128)S(1)} %pad_maximum_fusion.2), channel_id=1, replica_groups=mesh['gx'=8,'gy'=4,'gz'=8] {'gx','gy'}, use_global_device_ids=true, to_apply=%region_6.0 | all-reduce | flops 2560 | bytes 20480 | tf_op jit(solution)/shard_map/psum | solution.py:83
  507.8 1.7 fusion.8
  509.5 17.3 %all_gather.22 = bf16[384,640]{1,0:T(8,128)(2,1)S(1)} all-gather(bf16[48,640]{1,0:T(8,128)(2,1)S(1)} %get-tuple-element.33), channel_id=1, replica_groups=mesh['gx'=8,'gy'=4,'gz'=8] {'gx'}, dimensions={0}, use_global_device_ids=true | all-gather | bytes 552960 | tf_op jit(solution)/shard_map/all_gather | solution.py:85
  526.8 4.5 fusion.20
  531.3 61.7 %reduce-scatter.21.cloned.1.call-done = f32[48,1728]{1,0:T(8,128)} async-done(((f32[384,1728]{1,0:T(8,128)}), f32[48,1728]{1,0:T(8,128)}) %reduce-scatter.21.cloned.1.call-update) | async-done | bytes 331792 | tf_op jit(solution)/shard_map/reduce_scatter | solution.py:87
  593.0 1.2 multiply_convert_fusion.1
  594.2 0.8 pad_maximum_fusion.1
  595.1 3.5 fusion.22
  598.7 61.1 %all-gather.11.cloned.1.call-done = bf16[384,3456]{1,0:T(8,128)(2,1)} async-done(((bf16[48,3456]{1,0:T(8,128)(2,1)}), bf16[384,3456]{1,0:T(8,128)(2,1)}) %all-gather.11.cloned.1.call-update) | async-done | bytes 2654224 | tf_op jit(solution)/shard_map/all_gather | solution.py:97
  659.8 6.5 fusion.21
  666.6 5.1 convolution_bitcast_fusion
  671.6 10.5 %copy.32 = f32[640,3456]{1,0:T(8,128)} copy(f32[640,3456]{0,1:T(8,128)} %convolution_bitcast_fusion) | data formatting | bytes 17694720
  682.2 68.1 %reduce-scatter.17.cloned.1.call-done = f32[432,640]{1,0:T(8,128)} async-done(((f32[1728,640]{1,0:T(8,128)}), f32[432,640]{1,0:T(8,128)}) %reduce-scatter.17.cloned.1.call-update) | async-done | bytes 1105936 | tf_op jit(solution)/shard_map/reduce_scatter | solution.py:90
  750.3 2.1 convert_element_type.33
  752.4 31.0 %reduce-scatter.15.cloned.1.call-done = f32[48,640]{1,0:T(8,128)} async-done(((f32[384,640]{1,0:T(8,128)}), f32[48,640]{1,0:T(8,128)}) %reduce-scatter.15.cloned.1.call-update) | async-done | bytes 122896 | tf_op jit(solution)/shard_map/reduce_scatter | solution.py:100
  783.3 1.5 convert_element_type.32
  784.9 163.1 %reduce-scatter.23.cloned.1.call-done = f32[160,3456]{1,0:T(8,128)} async-done(((f32[640,3456]{1,0:T(8,128)}), f32[160,3456]{1,0:T(8,128)}) %reduce-scatter.23.cloned.1.call-update) | async-done | bytes 2211856
  947.9 2.3 copy.33
  950.3 1.1 copy.26
  951.4 1.1 copy.25
  (40 shorter events, 1.7 us)
Async XLA Ops:
  7.2 2.6 copy-start.3
  7.2 89.0 %all-gather.5.cloned.1.call-start = ((), (), s32[]{:S(2)}) async-start(), calls=%async_computation.6 | async-start | bytes 5529600 | tf_op jit(solution)/shard_map/all_gather | solution.py:61
  9.7 220.3 %reduce-scatter.19.cloned.1.call-start = ((), (), s32[]{:S(2)}) async-start(), calls=%async_computation.13 | async-start | bytes 5971968 | tf_op jit(solution)/shard_map/reduce_scatter | solution.py:64
  109.6 174.4 %all-gather.9.cloned.1.call-start = ((), (), s32[]{:S(2)}) async-start(), calls=%async_computation.8 | async-start | bytes 2764800 | tf_op jit(solution)/shard_map/all_gather | solution.py:76
  110.4 216.9 %all-gather.7.cloned.1.call-start = ((), (), s32[]{:S(2)}) async-start(), calls=%async_computation.7 | async-start | bytes 1548288 | tf_op jit(solution)/shard_map/all_gather | solution.py:75
  232.0 275.9 %copy-start.4 = (bf16[48,640]{1,0:T(8,128)(2,1)S(1)}, bf16[48,640]{1,0:T(8,128)(2,1)}, u32[]{:S(2)}) copy-start(bf16[48,640]{1,0:T(8,128)(2,1)} %param.10) | copy-start | bytes 184324
  232.0 275.9 %copy-start.5 = (f32[640]{0:T(1024)S(1)}, f32[640]{0:T(1024)}, u32[]{:S(2)}) copy-start(f32[640]{0:T(1024)} %param.11) | copy-start | bytes 7684
  232.0 133.9 %reduce-scatter.13.cloned.1.call-start = ((), (), s32[]{:S(2)}) async-start(), calls=%async_computation.9 | async-start | bytes 1105920 | tf_op jit(solution)/shard_map/reduce_scatter | solution.py:77
  331.6 261.4 %reduce-scatter.21.cloned.1.call-start = ((), (), s32[]{:S(2)}) async-start(), calls=%async_computation.14 | async-start | bytes 3096576 | tf_op jit(solution)/shard_map/reduce_scatter | solution.py:87
  531.2 61.8 %copy-start.1 = (f32[48,3456]{1,0:T(8,128)S(1)}, f32[48,3456]{1,0:T(8,128)}, u32[]{:S(2)}) copy-start(f32[48,3456]{1,0:T(8,128)} %reduce-scatter.19.cloned.1.call-done) | copy-start | bytes 1990660
  531.2 63.9 %copy-start.2 = (bf16[384,1728]{1,0:T(8,128)(2,1)S(1)}, bf16[384,1728]{1,0:T(8,128)(2,1)}, u32[]{:S(2)}) copy-start(bf16[384,1728]{1,0:T(8,128)(2,1)} %all-gather.7.cloned.1.call-done) | copy-start | bytes 3981316
  531.3 128.5 %all-gather.11.cloned.1.call-start = ((), (), s32[]{:S(2)}) async-start(), calls=%async_computation.10 | async-start | bytes 2985984 | tf_op jit(solution)/shard_map/all_gather | solution.py:97
  595.1 155.2 %reduce-scatter.17.cloned.1.call-start = ((), (), s32[]{:S(2)}) async-start(), calls=%async_computation.12 | async-start | bytes 5529600 | tf_op jit(solution)/shard_map/reduce_scatter | solution.py:90
  598.7 184.7 %reduce-scatter.15.cloned.1.call-start = ((), (), s32[]{:S(2)}) async-start(), calls=%async_computation.11 | async-start | bytes 1105920 | tf_op jit(solution)/shard_map/reduce_scatter | solution.py:100
  659.8 6.8 copy-start
  666.3 281.6 %reduce-scatter.23.cloned.1.call-start = ((), (), s32[]{:S(2)}) async-start(), calls=%async_computation.15 | async-start | bytes 11059200
Sparse Core Ops, SparseCore 0:
  9.8 86.2 all-gather.4
  109.7 120.2 reduce-scatter.18
  231.8 52.1 all-gather.8
  286.3 40.9 all-gather.6
  331.7 34.1 reduce-scatter.12
  531.4 61.5 reduce-scatter.20
  595.4 64.3 all-gather.10
  662.4 87.8 reduce-scatter.16
  753.0 30.2 reduce-scatter.14
  785.8 162.0 reduce-scatter.22
where the time goes:
time: 960 us; the launch traced here: 959 us
  waiting for transfers between devices  705 us (73%)
  blocking collectives  174 us (18%)
  matrix products  31.2 us (3%)
  local copies, waits for them, and re-layouts  21.2 us (2%)
  between operations  14.3 us (1%)
  other arithmetic  12.7 us (1%)
    unnamed x11, waiting for transfers between devices  164 us
    psum x1, blocking collectives, body(): totals = lax.psum(moment_sums(result), ('gx', 'gy'))  141 us
    reduce_scatter x1, waiting for transfers between devices, body(): lax.psum_scatter(jnp.dot(rows_in, both_weights, preferred_element_type=jn...  120 us
    all_gather x1, waiting for transfers between devices, body(): lax.all_gather(jnp.concatenate([gate_weight, up_weight], 1), 'gy', axis=0...  70.2 us
    reduce_scatter x1, waiting for transfers between devices, body(): lax.psum_scatter(contract_rows(hidden_rows, grad_rows), 'gy', scatter_dim...  68.1 us
    reduce_scatter x1, waiting for transfers between devices, body(): lax.psum_scatter(contract_columns(grad_rows, down_full), 'gz', scatter_di...  61.7 us
    all_gather x1, waiting for transfers between devices, body(): lax.all_gather(jnp.concatenate([grad_gate_act, grad_up_act], 1), 'gz', ax...  61.1 us
    all_gather x1, waiting for transfers between devices, body(): down_full = lax.all_gather(down_weight, 'gy', axis=0, tiled=True)  52 us
  transfers between devices with their start and end apart: 10, of which 10 were waited for; matrix products, arithmetic and copies ran while one was open for 3% of the time, Pallas kernels for 0%

commit v1 on v0

v1 whole, which is shorter than its diff:
```python
import jax
import jax.numpy as jnp
from jax import lax
from jax.experimental import pallas as pl
from jax.experimental.pallas import tpu as pltpu
from jax.sharding import PartitionSpec as P

EPSILON = 1e-05
BF, F32 = jnp.bfloat16, jnp.float32
NT = 1536.0
CO = (0, 512, 1024, 1536)
CW = (512, 512, 512, 256)


def dot(a, b):
    return lax.dot_general(a, b, (((1,), (0,)), ((), ())), preferred_element_type=F32)


def dot_t(a, b):
    return lax.dot_general(a, b, (((1,), (1,)), ((), ())), preferred_element_type=F32)


def t_dot(a, b):
    return lax.dot_general(a, b, (((0,), (0,)), ((), ())), preferred_element_type=F32)


def penalty_grad(values, totals, cotangent, weight):
    mean = totals[0:1] / NT
    two = totals[1:2] / NT
    three = totals[2:3] / NT
    four = totals[3:4] / NT
    c2 = two - mean * mean
    c3 = three - 3.0 * mean * two + 2.0 * mean * mean * mean
    c4 = four - 4.0 * mean * three + 6.0 * mean * mean * two - 3.0 * mean * mean * mean * mean
    v = c2 + EPSILON
    d = values - mean
    extra = (d * d * d - c3) / (v * v) - c4 * d / (v * v * v)
    return (cotangent.astype(F32) + weight * extra).astype(BF)


def wide(t, core):
    if t < 3:
        return pl.ds(pl.multiple_of(CO[t] + core * 256, 128), 256)
    return pl.ds(pl.multiple_of(CO[3] + core * 128, 128), 128)


def narrow(t):
    return pl.ds(t * 256, 256 if t < 3 else 128)


def kernel(
    s_ref, tok_ref, wd_ref, cot_ref, pw_ref,
    mixed_ref, dtok_ref, dw_out, gd_ref,
    wf, tokf, pre_s, pre_r, acc, pre2_s, pre2_r, gu,
    h_own, hidf, wdf, y_s, y_r, y2_s, y2_r, mom, mom_r, gyf,
    dh_s, dh_r, dh_p, gd_acc, gd_s, gd_r,
    dgf, dt_acc, dt_s, dt_r, dt2_s, dt2_r, dw_acc, dw_s, dw_r, dw_o,
    s_tz, s_tx, s_wz, s_wl, s_wc, s_py, s_pz, s_h, s_wd, s_wdl, s_yx, s_yz, s_m,
    s_gz, s_gx, s_dh, s_dhp, s_gd, s_gp, s_go, s_gf, s_dtx, s_dtz, s_dwc, s_dwz,
):
    gx, gy, gz = lax.axis_index("gx"), lax.axis_index("gy"), lax.axis_index("gz")
    x, c, zh, y, zl = gx // 2, gx % 2, gy, gz // 2, gz % 2

    def flip(a, k):
        if k == 1:
            return a + 1 - 2 * (a % 2)
        if k == 2:
            return (a + 2) % 4
        if k == 3:
            return 3 - a
        return a

    def dev(dx=0, dc=0, dy=0, dzh=0, dzl=0, zl_at=None):
        zz = zl_at if zl_at is not None else (1 - zl if dzl else zl)
        cc = 1 - c if dc else c
        return (flip(x, dx) * 2 + cc, flip(zh, dzh), flip(y, dy) * 2 + zz)

    pending = []

    def send(src, dst, ss, rs, to):
        cp = pltpu.make_async_remote_copy(
            src_ref=src, dst_ref=dst, send_sem=ss, recv_sem=rs,
            device_id=to, device_id_type=pl.DeviceIdType.MESH,
        )
        cp.start()
        pending.append(cp)
        return cp

    barrier = pltpu.get_barrier_semaphore()
    peers = [dev(dc=1)]
    peers += [dev(dx=d) for d in (1, 2, 3)]
    peers += [dev(dzh=e) for e in (1, 2, 3)]
    peers += [dev(dy=f, dzl=g) for f in range(4) for g in range(2) if (f, g) != (0, 0)]
    for p in peers:
        pl.semaphore_signal(barrier, inc=1, device_id=p, device_id_type=pl.DeviceIdType.MESH)
    pl.semaphore_wait(barrier, len(peers))

    tokf[0, 0] = tok_ref[...]
    tz = [send(tok_ref, tokf.at[e, 0], s_tz.at[0, e - 1], s_tz.at[1, e - 1], dev(dzh=e)) for e in (1, 2, 3)]
    wz, wl = [], []
    for t in range(4):
        cp = pltpu.make_async_copy(s_ref.at[zh, :, narrow(t)], wf.at[zh, :, wide(t, c)], s_wl.at[t])
        cp.start()
        wl.append(cp)
        wz.append([
            send(s_ref.at[flip(zh, e), :, narrow(t)], wf.at[zh, :, wide(t, c)],
                 s_wz.at[0, t, e - 1], s_wz.at[1, t, e - 1], dev(dzh=e))
            for e in (1, 2, 3)
        ])
    wdl, wdr = [], []
    for t in range(4):
        if t < 3:
            src, at = pl.ds(t * 128, 128), pl.ds(pl.multiple_of(t * 256 + c * 128, 16), 128)
        else:
            src, at = pl.ds(384, 48), pl.ds(pl.multiple_of(768 + c * 48, 16), 48)
        cp = pltpu.make_async_copy(wd_ref.at[src], wdf.at[at], s_wdl.at[t])
        cp.start()
        wdl.append(cp)
        wdr.append(send(wd_ref.at[src], wdf.at[at], s_wd.at[0, t], s_wd.at[1, t], dev(dc=1)))
    wdf[864:896, :] = jnp.zeros((32, 640), BF)
    for cp in tz:
        cp.wait_recv()
    tx = [send(tokf.at[:, 0], tokf.at[:, d], s_tx.at[0, d - 1], s_tx.at[1, d - 1], dev(dx=d)) for d in (1, 2, 3)]
    wc = []
    for t in range(4):
        wl[t].wait()
        for cp in wz[t]:
            cp.wait_recv()
        wc.append(send(wf.at[:, :, wide(t, c)], wf.at[:, :, wide(t, c)], s_wc.at[0, t], s_wc.at[1, t], dev(dc=1)))
    for cp in tx:
        cp.wait_recv()

    py, pz = [], []

    def matmul_pre(t):
        wc[t].wait_recv()
        cols = pl.ds(CO[t], CW[t])

        def step(i, _):
            w = wf[:, :, cols].reshape(640, CW[t])
            pre_s[i, :, cols] = dot(tokf[i].reshape(192, 640), w).astype(BF)
            return 0

        lax.fori_loop(0, 4, step, 0)
        py.append([
            send(pre_s.at[flip(y, f), :, cols], pre_r.at[f - 1, :, cols],
                 s_py.at[0, t, f - 1], s_py.at[1, t, f - 1], dev(dy=f))
            for f in (1, 2, 3)
        ])

    def sum_y(t):
        for cp in py[t]:
            cp.wait_recv()
        cols = pl.ds(CO[t], CW[t])

        def half(h):
            rows = pl.ds(pl.multiple_of(h * 96, 16), 96)
            return (
                pre_s[y, rows, cols].astype(F32) + pre_r[0, rows, cols].astype(F32)
            ) + (pre_r[1, rows, cols].astype(F32) + pre_r[2, rows, cols].astype(F32))

        pre2_s[:, cols] = half(1 - zl).astype(BF)
        pz.append(send(pre2_s.at[:, cols], pre2_r.at[:, cols], s_pz.at[0, t], s_pz.at[1, t], dev(dzl=1)))
        acc[:, cols] = half(zl)

    lane = lax.broadcasted_iota(jnp.int32, (96, 128), 1)

    def finish_pre(t):
        pz[t].wait_recv()
        cols = pl.ds(CO[t], CW[t])
        v = acc[:, cols] + pre2_r[:, cols].astype(F32)
        gu[:, cols] = v
        if t < 3:
            for k in range(2):
                g, u = v[:, k * 256 : k * 256 + 128], v[:, k * 256 + 128 : k * 256 + 256]
                h_own[:, t * 256 + k * 128 : t * 256 + k * 128 + 128] = (g * jax.nn.sigmoid(g) * u).astype(BF)
        else:
            hs = []
            for k in range(2):
                g = v[:, k * 128 : k * 128 + 128]
                hs.append(g * jax.nn.sigmoid(g) * pltpu.roll(g, 80, 1))
            tail = jnp.where(lane < 48, hs[0], jnp.where(lane < 96, pltpu.roll(hs[1], 48, 1), 0.0))
            h_own[:, 768:896] = tail.astype(BF)

    for t in range(6):
        if t < 4:
            matmul_pre(t)
        if 0 <= t - 1 < 4:
            sum_y(t - 1)
        if 0 <= t - 2 < 4:
            finish_pre(t - 2)

    hidf[y, zl] = h_own[...]
    hs = {}
    k = 0
    for f, g in ((0, 1), (1, 0), (1, 1), (3, 0), (3, 1), (2, 0), (2, 1)):
        hs[f, g] = send(h_own, hidf.at[y, zl], s_h.at[0, k], s_h.at[1, k], dev(dy=f, dzl=g))
        k += 1
    for cp in wdl:
        cp.wait()
    for cp in wdr:
        cp.wait_recv()

    def reduce_tokens(make_rows, s_buf, r_buf, s2_buf, r2_buf, sem_x, sem_z, order):
        xs = []
        for k, f in enumerate(order):
            e = flip(y, f)
            make_rows(f, e)
            for d in (1, 2, 3):
                xs.append(send(s_buf.at[e, d], r_buf.at[d - 1, e], sem_x.at[0, k, d - 1], sem_x.at[1, k, d - 1], dev(dx=d)))
        for cp in xs:
            cp.wait_recv()
        zs = []

        def total(e):
            return (s_buf[e, 0].astype(F32) + r_buf[0, e].astype(F32)) + (
                r_buf[1, e].astype(F32) + r_buf[2, e].astype(F32)
            )

        for e in (2, 1, 3):
            s2_buf[e - 1] = total(e).astype(BF)
            zs.append(send(s2_buf.at[e - 1], r2_buf.at[e - 1], sem_z.at[0, e - 1], sem_z.at[1, e - 1], dev(dzh=e)))
        own = total(0)
        for cp in zs:
            cp.wait_recv()
        return (own + r2_buf[0].astype(F32)) + (r2_buf[1].astype(F32) + r2_buf[2].astype(F32))

    def y_rows(f, e):
        for g in range(2):
            if (f, g) in hs:
                hs[f, g].wait_recv()
        yb = dot(hidf[e].reshape(192, 896), wdf[...])
        y_s[e] = yb.astype(BF).reshape(4, 48, 640)

    yv = reduce_tokens(y_rows, y_s, y_r, y2_s, y2_r, s_yx, s_yz, (0, 1, 3, 2))
    mixed_ref[...] = yv.astype(BF)

    sq = yv * yv
    mom[0, 0:4] = jnp.concatenate(
        [jnp.sum(v, 0, keepdims=True) for v in (yv, sq, sq * yv, sq * sq)], 0
    )
    mom[0, 4:8] = jnp.zeros((4, 640), F32)
    cp = send(mom.at[0], mom_r.at[0], s_m.at[0, 0], s_m.at[1, 0], dev(dc=1))
    cp.wait_recv()
    mom[1] = mom[0] + mom_r[0]
    cps = [send(mom.at[1], mom_r.at[d], s_m.at[0, d], s_m.at[1, d], dev(dx=d)) for d in (1, 2, 3)]
    for cp in cps:
        cp.wait_recv()
    mom[2] = (mom[1] + mom_r[1]) + (mom_r[2] + mom_r[3])
    cps = [send(mom.at[2], mom_r.at[3 + e], s_m.at[0, 3 + e], s_m.at[1, 3 + e], dev(dzh=e)) for e in (1, 2, 3)]
    for cp in cps:
        cp.wait_recv()
    totals = (mom[2] + mom_r[4]) + (mom_r[5] + mom_r[6])
    gyf[0, 0] = penalty_grad(yv, totals, cot_ref[...], pw_ref[...])

    cps = [send(gyf.at[0, 0], gyf.at[e, 0], s_gz.at[0, e - 1], s_gz.at[1, e - 1], dev(dzh=e)) for e in (1, 2, 3)]
    for cp in cps:
        cp.wait_recv()
    gxs = [send(gyf.at[:, 0], gyf.at[:, d], s_gx.at[0, d - 1], s_gx.at[1, d - 1], dev(dx=d)) for d in (1, 2, 3)]

    def dh_rows(d):
        if d:
            gxs[d - 1].wait_recv()
        v = dot_t(gyf[:, d].reshape(192, 640), wdf[...])
        dh_s[d // 2, :, (d % 2) * 48 : (d % 2) * 48 + 48, :] = v.astype(BF).reshape(4, 48, 896)

    dhs = []
    for p in range(2):
        dh_rows(2 * p)
        dh_rows(2 * p + 1)
        for f in (1, 2, 3):
            dhs.append(send(dh_s.at[p, flip(y, f)], dh_r.at[f - 1, zl],
                            s_dh.at[0, f - 1, p], s_dh.at[1, f - 1, zl], dev(dy=f, zl_at=p)))
    dhp = send(dh_s.at[1 - zl, y], dh_p, s_dhp.at[0], s_dhp.at[1], dev(dzl=1))

    def gd_part(core, t):
        if t < 3:
            h = hidf[:, :, :, pl.ds(pl.multiple_of(t * 256 + core * 128, 128), 128)].reshape(768, 128)
        else:
            h = hidf[:, :, :, 768:896].reshape(768, 128)
        return t_dot(h, gyf[...].reshape(768, 640))

    for t in range(3):
        gd_s[t * 128 : t * 128 + 128] = gd_part(1 - c, t).astype(BF)
    gd_acc[384:512] = gd_part(0, 3)
    gd_s[384:432] = gd_acc[pl.ds(pl.multiple_of(384 + (1 - c) * 48, 8), 48)].astype(BF)
    gdc = send(gd_s, gd_r, s_gd.at[0], s_gd.at[1], dev(dc=1))
    for t in range(3):
        gd_acc[t * 128 : t * 128 + 128] = gd_part(c, t)

    for f in (1, 2, 3):
        for p in range(2):
            pltpu.make_async_remote_copy(
                src_ref=dh_s.at[p, flip(y, f)], dst_ref=dh_r.at[f - 1, p],
                send_sem=s_dh.at[0, f - 1, p], recv_sem=s_dh.at[1, f - 1, p],
                device_id=dev(dy=f, zl_at=p), device_id_type=pl.DeviceIdType.MESH,
            ).wait_recv()
    dhp.wait_recv()

    def dh_at(lo):
        cols = pl.ds(lo, 128)
        v = dh_s[zl, y, :, cols].astype(F32) + dh_p[:, cols].astype(F32)
        for f in range(3):
            v = v + (dh_r[f, 0, :, cols].astype(F32) + dh_r[f, 1, :, cols].astype(F32))
        return v

    def gate_up_grads(dh, g, u):
        sg = jax.nn.sigmoid(g)
        return dh * u * sg * (1.0 + g * (1.0 - sg)), dh * (g * sg)

    gps, gos = [], []
    for t in range(4):
        base = CO[t]
        if t < 3:
            for k in range(2):
                lo = base + k * 256
                dg, du = gate_up_grads(
                    dh_at(t * 256 + k * 128), gu[:, lo : lo + 128], gu[:, lo + 128 : lo + 256]
                )
                dgf[y, zl, :, lo : lo + 128] = dg.astype(BF)
                dgf[y, zl, :, lo + 128 : lo + 256] = du.astype(BF)
        else:
            tail = dh_at(768)
            for k in range(2):
                lo = base + k * 128
                g = gu[:, lo : lo + 128]
                dh = tail if k == 0 else pltpu.roll(tail, 80, 1)
                dg, du = gate_up_grads(dh, g, pltpu.roll(g, 80, 1))
                v = jnp.where(lane < 48, dg, jnp.where(lane < 96, pltpu.roll(du, 48, 1), 0.0))
                dgf[y, zl, :, lo : lo + 128] = v.astype(BF)
        cols = pl.ds(CO[t], CW[t])
        own = dgf.at[y, zl, :, cols]
        gps.append(send(own, own, s_gp.at[0, t], s_gp.at[1, t], dev(dzl=1)))
        gos.append([send(own, own, s_go.at[0, t, f - 1], s_go.at[1, t, f - 1], dev(dy=f)) for f in (1, 2, 3)])

    gfs = []
    for t in range(4):
        cols = pl.ds(CO[t], CW[t])
        gps[t].wait_recv()
        other = dgf.at[y, 1 - zl, :, cols]
        gfs.append([send(other, other, s_gf.at[0, t, f - 1], s_gf.at[1, t, f - 1], dev(dy=f)) for f in (1, 2, 3)])

    gdc.wait_recv()
    gd_ref[0:384] = (gd_acc[0:384] + gd_r[0:384].astype(F32)).astype(BF)
    gd_ref[384:432] = (
        gd_acc[pl.ds(pl.multiple_of(384 + c * 48, 8), 48)] + gd_r[384:432].astype(F32)
    ).astype(BF)

    dwc, dwz = [], []

    def grads_chunk(t):
        for cp in gos[t]:
            cp.wait_recv()
        for cp in gfs[t]:
            cp.wait_recv()
        cols = pl.ds(CO[t], CW[t])
        nc = CW[t] // 2
        for core, buf in ((1 - c, dw_s), (c, dw_acc)):
            v = t_dot(tokf[...].reshape(768, 640), dgf[:, :, :, wide(t, core)].reshape(768, nc))
            buf[:, narrow(t)] = v.astype(buf.dtype)
            if buf is dw_s:
                dwc.append(send(dw_s.at[:, narrow(t)], dw_r.at[:, narrow(t)], s_dwc.at[0, t], s_dwc.at[1, t], dev(dc=1)))

        def step(i, _):
            w = wf[:, :, cols].reshape(640, CW[t])
            v = dot_t(dgf[i, :, :, cols].reshape(192, CW[t]), w)
            dt_acc[i] = v if t == 0 else dt_acc[i] + v
            return 0

        lax.fori_loop(0, 4, step, 0)

    def send_dw(t):
        dwc[t].wait_recv()
        at = narrow(t)
        v = (dw_acc[:, at] + dw_r[:, at].astype(F32)).astype(BF)
        dw_o[:, :, at] = v.reshape(4, 160, v.shape[1])
        cp = pltpu.make_async_copy(dw_o.at[zh, :, at], dw_out.at[zh, :, at], s_wl.at[t])
        cp.start()
        wl2.append(cp)
        dwz.append([
            send(dw_o.at[flip(zh, e), :, at], dw_out.at[zh, :, at],
                 s_dwz.at[0, t, e - 1], s_dwz.at[1, t, e - 1], dev(dzh=e))
            for e in (1, 2, 3)
        ])

    wl2 = []
    for t in range(4):
        grads_chunk(t)
        send_dw(t)

    def dt_rows(f, e):
        dt_s[e] = dt_acc[e].astype(BF).reshape(4, 48, 640)

    dtv = reduce_tokens(dt_rows, dt_s, dt_r, dt2_s, dt2_r, s_dtx, s_dtz, (0, 1, 3, 2))
    dtok_ref[...] = dtv.astype(BF)
    for t in range(4):
        wl2[t].wait()
        for cp in dwz[t]:
            cp.wait_recv()
    for cp in pending:
        cp.wait_send()


def body(tokens, gate_weight, up_weight, down_weight, cotangent, penalty_weight):
    pieces = []
    zero = jnp.zeros((160, 32), BF)
    for j in range(4):
        g = gate_weight[:, 432 * j : 432 * j + 432]
        u = up_weight[:, 432 * j : 432 * j + 432]
        parts = []
        for t in range(3):
            parts += [g[:, 128 * t : 128 * t + 128], u[:, 128 * t : 128 * t + 128]]
        pieces.append(jnp.concatenate(parts + [g[:, 384:], u[:, 384:], zero], 1))
    staged = jnp.stack(pieces)
    V, D = pltpu.VMEM, pltpu.SemaphoreType.DMA
    scratch = [
        V((4, 160, 1792), BF), V((4, 4, 48, 640), BF), V((4, 192, 1792), BF), V((3, 192, 1792), BF),
        V((96, 1792), F32), V((96, 1792), BF), V((96, 1792), BF), V((96, 1792), F32),
        V((96, 896), BF), V((4, 2, 96, 896), BF), V((896, 640), BF),
        V((4, 4, 48, 640), BF), V((3, 4, 48, 640), BF), V((3, 48, 640), BF), V((3, 48, 640), BF),
        V((3, 8, 640), F32), V((7, 8, 640), F32), V((4, 4, 48, 640), BF),
        V((2, 4, 96, 896), BF), V((3, 2, 96, 896), BF), V((96, 896), BF),
        V((512, 640), F32), V((432, 640), BF), V((432, 640), BF),
        V((4, 2, 96, 1792), BF), V((4, 192, 640), F32),
        V((4, 4, 48, 640), BF), V((3, 4, 48, 640), BF), V((3, 48, 640), BF), V((3, 48, 640), BF),
        V((640, 896), F32), V((640, 896), BF), V((640, 896), BF), V((4, 160, 896), BF),
        D((2, 3)), D((2, 3)), D((2, 4, 3)), D((4,)), D((2, 4)), D((2, 4, 3)), D((2, 4)), D((2, 7)),
        D((2, 4)), D((4,)), D((2, 4, 3)), D((2, 3)), D((2, 7)),
        D((2, 3)), D((2, 3)), D((2, 3, 2)), D((2,)), D((2,)), D((2, 4)), D((2, 4, 3)), D((2, 4, 3)),
        D((2, 4, 3)), D((2, 3)), D((2, 4)), D((2, 4, 3)),
    ]
    S = jax.ShapeDtypeStruct
    in_vmem = pl.BlockSpec(memory_space=pltpu.VMEM)
    mixed, grad_tokens, dw, grad_down = pl.pallas_call(
        kernel,
        out_shape=[S((48, 640), BF), S((48, 640), BF), S((4, 160, 896), BF), S((432, 640), BF)],
        in_specs=[in_vmem] * 5,
        out_specs=[in_vmem] * 4,
        scratch_shapes=scratch,
        compiler_params=pltpu.CompilerParams(
            collective_id=0, has_side_effects=True, vmem_limit_bytes=58 * 2**20
        ),
        cost_estimate=pl.CostEstimate(flops=8 * 10**9, bytes_accessed=6 * 10**6, transcendentals=0),
        name="ffn",
    )(staged, tokens, down_weight, cotangent, penalty_weight.reshape(1, 640))

    def assemble(first):
        parts = []
        for j in range(4):
            parts += [dw[j, :, 256 * t + 128 * first : 256 * t + 128 * first + 128] for t in range(3)]
            parts.append(dw[j, :, 768 + 48 * first : 816 + 48 * first])
        return jnp.concatenate(parts, 1)

    return (mixed, grad_tokens, assemble(0), assemble(1), grad_down)


def solution(mesh):
    in_specs = (
        P(("gy", "gx"), "gz"),
        P(("gz", "gy"), "gx"),
        P(("gz", "gy"), "gx"),
        P(("gx", "gy"), "gz"),
        P(("gy", "gx"), "gz"),
        P("gz"),
    )
    out_specs = (
        P(("gy", "gx"), "gz"),
        P(("gy", "gx"), "gz"),
        P(("gz", "gy"), "gx"),
        P(("gz", "gy"), "gx"),
        P(("gx", "gy"), "gz"),
    )
    return jax.shard_map(body, mesh=mesh, in_specs=in_specs, out_specs=out_specs, check_vma=False)
```

time: 960 us -> 229 us (0.24)
  waiting for transfers between devices: 705 us -> 0 us
  Pallas kernels: 0 us -> 212 us
  blocking collectives: 174 us -> 0 us
  matrix products: 31.2 us -> 0 us
  between operations: 14.3 us -> 0.74 us
  other arithmetic: 12.7 us -> 1.19 us
    reduce_scatter x5 -> x0, waiting for transfers between devices: 315 us -> none  [the longest x1 120 us: body(): lax.psum_scatter(jnp.dot(rows_in, both_weights, preferred_element_type=jn...]
    all_gather x4 -> x0, waiting for transfers between devices: 227 us -> none  [the longest x1 70.2 us: body(): lax.all_gather(jnp.concatenate([gate_weight, up_weight], 1), 'gy', axis=0...]
    pallas_call x0 -> x1, Pallas kernels: none -> 212 us  [body(): pl.pallas_call(kernel, out_shape=[S((48, 640), BF), S((48, 640), BF), S((...]
    unnamed x11 -> x0, waiting for transfers between devices: 164 us -> none
    psum x1 -> x0, blocking collectives: 141 us -> none  [body(): totals = lax.psum(moment_sums(result), ('gx', 'gy'))]
    all_gather x2 -> x0, blocking collectives: 33.4 us -> none  [the longest x1 17.3 us: body(): grad_rows = lax.all_gather(grad_own, 'gx', axis=0, tiled=True)]
    dot_general x5 -> x0, matrix products: 26.7 us -> none  [the longest x2 8.6 us: contract_rows(): lax.dot_general(left, right, (((0,), (0,)), ((), ())), preferred_element_...]
    unnamed x17 -> x11, local copies, waits for them, and re-layouts: 21.1 us -> 2.07 us
  transfers between devices with their start and end apart: 10 -> 0, of which waited for: 10 -> 0; matrix products, arithmetic and copies ran while one was open for 3% -> 0% of each run, Pallas kernels for 0% -> 0%
where the time goes in v1:
time: 229 us; the launch traced here: 226 us
  Pallas kernels  212 us (93%)
  local copies, waits for them, and re-layouts  12.2 us (5%)
    pallas_call x1, Pallas kernels, body(): pl.pallas_call(kernel, out_shape=[S((48, 640), BF), S((48, 640), BF), S((...  212 us

profile of v1, /device:TPU:1, one launch (start us, length us, event | category | flops | bytes accessed | tf_op | source)
XLA Modules:
  0.0 226.0 jit_solution(5047115538851735097)
XLA Ops:
  0.6 0.0 copy-start
  0.6 1.3 reshape.13.pw_ref
  2.0 1.2 fusion
  3.2 1.4 fusion.3
  4.6 0.0 copy-done
  4.6 0.2 fusion.2
  4.8 0.1 concatenate.18
  4.9 0.1 concatenate.21
  5.1 0.1 concatenate.20
  5.2 0.1 concatenate.19
  5.3 1.2 pad_maximum_fusion.s_ref
  6.5 211.9 %ffn.1 = (bf16[48,640]{1,0:T(8,128)(2,1)}, bf16[48,640]{1,0:T(8,128)(2,1)}, bf16[4,160,896]{2,1,0:T(8,128)(2,1)}, bf16[432,640]{1,0:T(8,128)(2,1)}) custom-call(bf16[4,160,896]{2,1,0:T(8,128)(2,1)} %pad_maximum_fusion.s_ref, bf16[48,640]{1,0:T(8,128)(2,1)} %tok_ref.1, bf16[432,640]{1,0:T(8,128)(2,1)} %wd_ref.1, bf16[48,640]{1,0:T(8,128)(2,1)} %cot_ref.1, ...), custom_call_target="tpu_custom_call" | custom-call | flops 8000000000 | bytes 6000000 | tf_op jit(solution)/shard_map/ffn/pallas_call | solution.py:434
  218.4 0.9 slice_bitcast_fusion.26
  219.3 1.1 slice_bitcast_fusion
  220.4 1.2 slice_bitcast_fusion.1
  221.6 0.0 copy-start.3
  221.7 0.0 copy-start.2
  221.7 0.0 copy-start.1
  221.7 1.2 concatenate.23
  222.8 1.1 concatenate.22
  224.0 0.0 copy-done.3
  224.0 0.6 copy.14
  224.6 0.0 copy-done.2
  224.6 0.6 copy.15
  225.2 0.0 copy-done.1
  225.2 0.8 copy.16
  (1 shorter events, 0.0 us)
Async XLA Ops:
  0.6 4.0 %copy-start = (bf16[160,1728]{1,0:T(8,128)(2,1)S(1)}, bf16[160,1728]{1,0:T(8,128)(2,1)}, u32[]{:S(2)}) copy-start(bf16[160,1728]{1,0:T(8,128)(2,1)} %param.8) | copy-start | bytes 1658884
  221.6 2.3 %copy-start.3 = (bf16[48,640]{1,0:T(8,128)(2,1)S(1)}, bf16[48,640]{1,0:T(8,128)(2,1)}, u32[]{:S(2)}) copy-start(bf16[48,640]{1,0:T(8,128)(2,1)} %get-tuple-element.86) | copy-start | bytes 184324
  221.7 2.9 %copy-start.2 = (bf16[48,640]{1,0:T(8,128)(2,1)S(1)}, bf16[48,640]{1,0:T(8,128)(2,1)}, u32[]{:S(2)}) copy-start(bf16[48,640]{1,0:T(8,128)(2,1)} %get-tuple-element.87) | copy-start | bytes 184324
  221.7 3.6 %copy-start.1 = (bf16[432,640]{1,0:T(8,128)(2,1)S(1)}, bf16[432,640]{1,0:T(8,128)(2,1)}, u32[]{:S(2)}) copy-start(bf16[432,640]{1,0:T(8,128)(2,1)} %get-tuple-element.90) | copy-start | bytes 1658884

commit v2 on v1

v2 whole, which is shorter than its diff:
```python
import jax
import jax.numpy as jnp
from jax import lax
from jax.experimental import pallas as pl
from jax.experimental.pallas import tpu as pltpu
from jax.sharding import PartitionSpec as P

EPSILON = 1e-05
BF, F32 = jnp.bfloat16, jnp.float32
NT = 1536.0
CO = (0, 512, 1024, 1536)
CW = (512, 512, 512, 256)
SLOTS = 64


def dot(a, b):
    return lax.dot_general(a, b, (((1,), (0,)), ((), ())), preferred_element_type=F32)


def dot_t(a, b):
    return lax.dot_general(a, b, (((1,), (1,)), ((), ())), preferred_element_type=F32)


def t_dot(a, b):
    return lax.dot_general(a, b, (((0,), (0,)), ((), ())), preferred_element_type=F32)


def penalty_grad(values, totals, cotangent, weight):
    mean = totals[0:1] / NT
    two = totals[1:2] / NT
    three = totals[2:3] / NT
    four = totals[3:4] / NT
    c2 = two - mean * mean
    c3 = three - 3.0 * mean * two + 2.0 * mean * mean * mean
    c4 = four - 4.0 * mean * three + 6.0 * mean * mean * two - 3.0 * mean * mean * mean * mean
    v = c2 + EPSILON
    d = values - mean
    extra = (d * d * d - c3) / (v * v) - c4 * d / (v * v * v)
    return (cotangent.astype(F32) + weight * extra).astype(BF)


def cube_root(q):
    r = jnp.exp(jnp.log(jnp.abs(q)) * (1.0 / 3.0))
    return jnp.where(q < 0.0, -r, r)


def wide(t, core):
    if t < 3:
        return pl.ds(pl.multiple_of(CO[t] + core * 256, 128), 256)
    return pl.ds(pl.multiple_of(CO[3] + core * 128, 128), 128)


def narrow(t):
    return pl.ds(t * 256, 256 if t < 3 else 128)


def kernel(
    gw_ref, uw_ref, tok_ref, wd_ref, cot_ref, pw_ref,
    mixed_ref, dtok_ref, dg_ref, du_ref, gd_ref,
    gw, uw, mix, dt_o, gd_o, s_ref, wf, tokf, pre_h, pre_hr, pre_f, pre_s, pre_r, pre_own, acc, pre2_s, pre2_r,
    abf, hidf, wdf, y_own, y_s, y_r, y2_s, y2_r, mom, mom_r, mxf, cotf, gyf,
    dh_s, dh_r, dh_p, gd_acc, gd_s, gd_r, dhf,
    dgf, dt_acc, dt_own, dt_s, dt_r, dt2_s, dt2_r, dw_acc, dw_s, dw_r, dw_o, dw_f,
    s_send, s_in, s_out, s_tz, s_tx, s_wz, s_wl, s_wc, s_ph, s_py, s_pz, s_h, s_wd, s_wdl, s_yx, s_yz, s_m,
    s_gz, s_gx, s_cz, s_cx, s_ab, s_dh, s_dhp, s_gd, s_go, s_g0, s_g1, s_g2, s_dtx, s_dtz, s_dwc, s_dwz,
):
    gx, gy, gz = lax.axis_index("gx"), lax.axis_index("gy"), lax.axis_index("gz")
    x, c, zh, y, zl = gx // 2, gx % 2, gy, gz // 2, gz % 2

    def flip(a, k):
        if k == 1:
            return a + 1 - 2 * (a % 2)
        if k == 2:
            return (a + 2) % 4
        if k == 3:
            return 3 - a
        return a

    def dev(dx=0, dc=0, dy=0, dzh=0, dzl=0, zl_at=None):
        zz = zl_at if zl_at is not None else (1 - zl if dzl else zl)
        cc = 1 - c if dc else c
        return (flip(x, dx) * 2 + cc, flip(zh, dzh), flip(y, dy) * 2 + zz)

    pending, started = {}, [0]

    def send(src, dst, rs, to):
        slot = started[0] % SLOTS
        started[0] += 1
        if slot in pending:
            pending.pop(slot).wait_send()
        cp = pltpu.make_async_remote_copy(
            src_ref=src, dst_ref=dst, send_sem=s_send.at[slot], recv_sem=rs,
            device_id=to, device_id_type=pl.DeviceIdType.MESH,
        )
        cp.start()
        pending[slot] = cp
        return cp

    def sent(cps):
        for slot in [k for k, cp in pending.items() if any(cp is other for other in cps)]:
            pending.pop(slot).wait_send()

    barrier = pltpu.get_barrier_semaphore()
    peers = [dev(dx=d, dc=k) for d in range(4) for k in range(2) if (d, k) != (0, 0)]
    peers += [dev(dzh=e) for e in (1, 2, 3)]
    peers += [dev(dy=f, dzl=g) for f in range(4) for g in range(2) if (f, g) != (0, 0)]
    for p in peers:
        pl.semaphore_signal(barrier, inc=1, device_id=p, device_id_type=pl.DeviceIdType.MESH)
    ins = [
        pltpu.make_async_copy(src, to, s_in.at[k])
        for k, (src, to) in enumerate(((tok_ref, tokf.at[0, 0]), (gw_ref, gw), (uw_ref, uw), (cot_ref, cotf.at[0, 0])))
    ]
    for cp in ins:
        cp.start()
    lane160 = lax.broadcasted_iota(jnp.int32, (160, 128), 1)

    def shifted(ref, lo, at):
        base = lo // 128 * 128
        v = ref[:, base : min(base + 256, 1728)].astype(F32)
        if v.shape[1] < 256:
            v = jnp.concatenate([v, jnp.zeros((160, 256 - v.shape[1]), F32)], 1)
        r = (at - (lo - base)) % 256
        return (pltpu.roll(v, r, 1) if r else v)[:, 0:128]

    def stage(t):
        for j in range(4):
            if t < 3:
                for k, ref in enumerate((gw, uw)):
                    s_ref[j, :, t * 256 + k * 128 : t * 256 + k * 128 + 128] = shifted(ref, 432 * j + 128 * t, 0).astype(BF)
            else:
                g, u = shifted(gw, 432 * j + 384, 0), shifted(uw, 432 * j + 384, 48)
                s_ref[j, :, 768:896] = jnp.where(lane160 < 48, g, jnp.where(lane160 < 96, u, 0.0)).astype(BF)

    for cp in ins:
        cp.wait()
    stage(0)
    pl.semaphore_wait(barrier, len(peers))

    tz = [send(tokf.at[0, 0], tokf.at[e, 0], s_tz.at[e - 1], dev(dzh=e)) for e in (1, 3, 2)]
    wz, wl, wc = [], [], []

    def issue_w(t):
        cp = pltpu.make_async_copy(s_ref.at[zh, :, narrow(t)], wf.at[zh, :, wide(t, c)], s_wl.at[t])
        cp.start()
        wl.append(cp)
        wz.append([
            send(s_ref.at[flip(zh, e), :, narrow(t)], wf.at[zh, :, wide(t, c)],
                 s_wz.at[t, e - 1], dev(dzh=e))
            for e in (2, 1, 3)
        ])

    def forward_w(t):
        wl[t].wait()
        for cp in wz[t]:
            cp.wait_recv()
        wc.append(send(wf.at[:, :, wide(t, c)], wf.at[:, :, wide(t, c)], s_wc.at[t], dev(dc=1)))

    tx = [send(tokf.at[0, 0], tokf.at[0, d], s_tx.at[d - 1], dev(dx=d)) for d in (2, 1, 3)]
    stage(1)
    sent(tz)
    issue_w(0)
    stage(2)
    for e, cp in zip((1, 3, 2), tz):
        cp.wait_recv()
        tx += [send(tokf.at[e, 0], tokf.at[e, d], s_tx.at[3 * e + d - 1], dev(dx=d)) for d in (2, 1, 3)]
    stage(3)
    wdl, wdr = [], []
    for t in range(4):
        if t < 3:
            src, at = pl.ds(t * 128, 128), pl.ds(pl.multiple_of(t * 256 + c * 128, 16), 128)
        else:
            src, at = pl.ds(384, 48), pl.ds(pl.multiple_of(768 + c * 48, 16), 48)
        cp = pltpu.make_async_copy(wd_ref.at[src], wdf.at[at], s_wdl.at[t])
        cp.start()
        wdl.append(cp)
        wdr.append(send(wd_ref.at[src], wdf.at[at], s_wd.at[t], dev(dc=1)))
    wdf[864:896, :] = jnp.zeros((32, 640), BF)

    py, pz = [], []

    halves = []

    def matmul_pre(t):
        wc[t].wait_recv()
        cols = pl.ds(CO[t], CW[t])
        for f in (2, 1, 3, 0):
            w = wf[:, :, cols].reshape(640, CW[t])
            v = dot(tokf[flip(y, f)].reshape(192, 640), w)
            if f == 2:
                pre_h[:, cols] = v.astype(BF)
                halves.append([
                    send(pre_h.at[96 * k : 96 * k + 96, cols], pre_hr.at[k, :, cols], s_ph.at[t, k],
                         dev(dy=1 + 2 * k))
                    for k in range(2)
                ])
            elif f:
                pre_f[f // 2, :, cols] = v
            else:
                pre_own[:, cols] = v

    def relay(t):
        for cp in halves[t]:
            cp.wait_recv()
        cols = pl.ds(CO[t], CW[t])
        pre_s[0, 0:96, cols] = pre_f[0, 0:96, cols].astype(BF)
        pre_s[0, 96:192, cols] = (pre_f[0, 96:192, cols] + pre_hr[1, :, cols].astype(F32)).astype(BF)
        pre_s[1, 0:96, cols] = (pre_f[1, 0:96, cols] + pre_hr[0, :, cols].astype(F32)).astype(BF)
        pre_s[1, 96:192, cols] = pre_f[1, 96:192, cols].astype(BF)
        py.append([
            send(pre_s.at[k, :, cols], pre_r.at[k, :, cols], s_py.at[t, k], dev(dy=1 + 2 * k))
            for k in range(2)
        ])

    def sum_y(t):
        for cp in py[t]:
            cp.wait_recv()
        cols = pl.ds(CO[t], CW[t])

        def half(h):
            rows = pl.ds(pl.multiple_of(h * 96, 16), 96)
            return pre_own[rows, cols] + (pre_r[0, rows, cols].astype(F32) + pre_r[1, rows, cols].astype(F32))

        other = half(1 - zl)
        pre2_s[:, cols] = (other * other * other).astype(BF)
        pz.append(send(pre2_s.at[:, cols], pre2_r.at[:, cols], s_pz.at[t], dev(dzl=1)))
        acc[:, cols] = half(zl)

    lane = lax.broadcasted_iota(jnp.int32, (96, 128), 1)

    def factors(g, u):
        sg = jax.nn.sigmoid(g)
        act = g * sg
        return act * u, u * sg * (1.0 + g * (1.0 - sg)), act

    def finish_pre(t):
        pz[t].wait_recv()
        cols = pl.ds(CO[t], CW[t])
        v = acc[:, cols] + cube_root(pre2_r[:, cols].astype(F32))
        if t < 3:
            for k in range(2):
                h, fa, fb = factors(v[:, k * 256 : k * 256 + 128], v[:, k * 256 + 128 : k * 256 + 256])
                lo = CO[t] + k * 256
                hidf[y, zl, :, t * 256 + k * 128 : t * 256 + k * 128 + 128] = h.astype(BF)
                abf[y, zl, :, lo : lo + 128] = fa.astype(BF)
                abf[y, zl, :, lo + 128 : lo + 256] = fb.astype(BF)
        else:
            hs = []
            for k in range(2):
                g = v[:, k * 128 : k * 128 + 128]
                h, fa, fb = factors(g, pltpu.roll(g, 80, 1))
                hs.append(h)
                lo = CO[3] + k * 128
                abf[y, zl, :, lo : lo + 128] = jnp.where(
                    lane < 48, fa, jnp.where(lane < 96, pltpu.roll(fb, 48, 1), 0.0)
                ).astype(BF)
            tail = jnp.where(lane < 48, hs[0], jnp.where(lane < 96, pltpu.roll(hs[1], 48, 1), 0.0))
            hidf[y, zl, :, 768:896] = tail.astype(BF)

    sent(wz[0])
    issue_w(1)
    forward_w(0)
    for cp in tx:
        cp.wait_recv()
    matmul_pre(0)
    sent(wz[1])
    issue_w(2)
    forward_w(1)
    matmul_pre(1)
    relay(0)
    sent(wz[2])
    issue_w(3)
    forward_w(2)
    cz = [send(cotf.at[0, 0], cotf.at[e, 0], s_cz.at[e - 1], dev(dzh=e)) for e in (2, 1, 3)]
    matmul_pre(2)
    relay(1)
    sum_y(0)
    forward_w(3)
    relay(2)
    matmul_pre(3)
    sum_y(1)
    relay(3)
    finish_pre(0)
    sum_y(2)
    for cp in cz:
        cp.wait_recv()
    cxs = [send(cotf.at[:, 0], cotf.at[:, d], s_cx.at[d - 1], dev(dx=d)) for d in (2, 1, 3)]
    sum_y(3)
    finish_pre(1)
    finish_pre(2)
    finish_pre(3)

    class Gather:
        def __init__(self, ref, sems, cols):
            self.ref, self.sems, self.cols, self.cps = ref, sems, cols, {}

        def go(self, k, a, b, to, rows=pl.ds(0, 96)):
            block = self.ref.at[a, b, rows, self.cols]
            self.cps[k] = send(block, block, self.sems.at[k], to)

        def start_z(self):
            self.go(0, y, zl, dev(dzl=1))

        def start(self):
            for k in range(2):
                self.go(1 + k, y, zl, dev(dy=1 + 2 * k))

        def neighbour(self):
            self.cps[0].wait_recv()
            for k in range(2):
                self.go(3 + k, y, 1 - zl, dev(dy=1 + 2 * k))

        def onward(self, g):
            for k in range(2):
                self.cps[1 + 2 * g + k].wait_recv()
                z = 1 - zl if g else zl
                self.go(5 + 2 * g + k, flip(y, 1 + 2 * k), z, dev(dy=3 - 2 * k), pl.ds(48 * k, 48))

        def finish(self):
            for k in range(5, 9):
                self.cps[k].wait_recv()

    hid = Gather(hidf, s_h, pl.ds(0, 896))
    hid.start_z()
    hid.start()
    for cp in wdl:
        cp.wait()
    for cp in wdr:
        cp.wait_recv()
    hid.neighbour()
    ab = Gather(abf, s_ab, pl.ds(0, 1792))
    ab.start_z()

    def reduce_tokens(make_rows, own_buf, s_buf, r_buf, s2_buf, r2_buf, sem_x, sem_z, order, between=None):
        xs = []
        for k, f in enumerate(order):
            e = flip(y, f)
            v = make_rows(f, e).reshape(4, 48, 640)
            own_buf[e] = v[0]
            s_buf[e] = v[1:4].astype(BF)
            for d in (2, 1, 3):
                xs.append(send(s_buf.at[e, d - 1], r_buf.at[d - 1, e], sem_x.at[k, d - 1], dev(dx=d)))
        if between is not None:
            between()
        for cp in xs:
            cp.wait_recv()
        zs = []

        def total(e):
            return (own_buf[e] + r_buf[0, e].astype(F32)) + (
                r_buf[1, e].astype(F32) + r_buf[2, e].astype(F32)
            )

        for e in (2, 1, 3):
            s2_buf[e - 1] = total(e).astype(BF)
            zs.append(send(s2_buf.at[e - 1], r2_buf.at[e - 1], sem_z.at[e - 1], dev(dzh=e)))
        own = total(0)
        for cp in zs:
            cp.wait_recv()
        return (own + r2_buf[0].astype(F32)) + (r2_buf[1].astype(F32) + r2_buf[2].astype(F32))

    def y_rows(f, e):
        if f == 1:
            hid.onward(0)
            hid.onward(1)
        elif f == 2:
            hid.finish()
        return dot(hidf[e].reshape(192, 896), wdf[...])

    def after_y():
        ab.start()
        ab.neighbour()

    yv = reduce_tokens(y_rows, y_own, y_s, y_r, y2_s, y2_r, s_yx, s_yz, (0, 1, 3, 2), after_y)

    sq = yv * yv
    mom[0, 0:4] = jnp.concatenate(
        [jnp.sum(v, 0, keepdims=True) for v in (yv, sq, sq * yv, sq * sq)], 0
    )
    mom[0, 4:8] = jnp.zeros((4, 640), F32)
    cps = [
        send(mom.at[0], mom_r.at[2 * d + k - 1], s_m.at[2 * d + k - 1], dev(dx=d, dc=k))
        for d in (2, 1, 3, 0) for k in (1, 0) if (d, k) != (0, 0)
    ]
    mxf[0, 0] = (sq * yv).astype(BF)
    mz = [send(mxf.at[0, 0], mxf.at[e, 0], s_gz.at[e - 1], dev(dzh=e)) for e in (1, 3, 2)]
    mx = {d: [send(mxf.at[0, 0], mxf.at[0, d], s_gx.at[d - 1], dev(dx=d))] for d in (2, 1, 3)}
    mix[...] = yv.astype(BF)
    outs = [pltpu.make_async_copy(mix, mixed_ref, s_out.at[0])]
    outs[0].start()
    for cp in cps:
        cp.wait_recv()
    mom[1] = ((mom[0] + mom_r[0]) + (mom_r[1] + mom_r[2])) + ((mom_r[3] + mom_r[4]) + (mom_r[5] + mom_r[6]))
    ms = [send(mom.at[1], mom_r.at[6 + e], s_m.at[6 + e], dev(dzh=e)) for e in (2, 1, 3)]
    for e, cp in zip((1, 3, 2), mz):
        cp.wait_recv()
        for d in (2, 1, 3):
            mx[d].append(send(mxf.at[e, 0], mxf.at[e, d], s_gx.at[3 * e + d - 1], dev(dx=d)))
    ab.onward(0)
    ab.onward(1)
    for cp in ms:
        cp.wait_recv()
    mom[2] = (mom[1] + mom_r[7]) + (mom_r[8] + mom_r[9])
    for cp in cxs:
        cp.wait_recv()

    def dh_rows(d):
        if d:
            for cp in mx[d]:
                cp.wait_recv()
        totals, weight = mom[2], pw_ref[...].reshape(1, 640)
        for e in range(4):
            gyf[e, d] = penalty_grad(cube_root(mxf[e, d].astype(F32)), totals, cotf[e, d], weight)
        v = dot_t(gyf[:, d].reshape(192, 640), wdf[...])
        dh_s[d // 2, :, (d % 2) * 48 : (d % 2) * 48 + 48, :] = v.astype(BF).reshape(4, 48, 896)

    for d in (0, 1, 3, 2):
        dh_rows(d)
        p, q = d // 2, d % 2
        rows = pl.ds(48 * q, 48)
        for f in (2, 1, 3):
            send(dh_s.at[p, flip(y, f), rows], dh_r.at[f - 1, zl, rows],
                 s_dh.at[f - 1, zl, q], dev(dy=f, zl_at=p))
    dhp = send(dh_s.at[1 - zl, y], dh_p, s_dhp.at[0], dev(dzl=1))

    def gd_part(core, t):
        if t < 3:
            h = hidf[:, :, :, pl.ds(pl.multiple_of(t * 256 + core * 128, 128), 128)].reshape(768, 128)
        else:
            h = hidf[:, :, :, 768:896].reshape(768, 128)
        return t_dot(h, gyf[...].reshape(768, 640))

    for t in range(3):
        gd_s[t * 128 : t * 128 + 128] = gd_part(1 - c, t).astype(BF)
    gd_acc[384:512] = gd_part(0, 3)
    gd_s[384:432] = gd_acc[pl.ds(pl.multiple_of(384 + (1 - c) * 48, 8), 48)].astype(BF)
    gdc = send(gd_s, gd_r, s_gd.at[0], dev(dc=1))
    for t in range(3):
        gd_acc[t * 128 : t * 128 + 128] = gd_part(c, t)

    for f in (1, 2, 3):
        for p in range(2):
            for q in range(2):
                rows = pl.ds(48 * q, 48)
                pltpu.make_async_remote_copy(
                    src_ref=dh_s.at[p, flip(y, f), rows], dst_ref=dh_r.at[f - 1, p, rows],
                    send_sem=s_send.at[0], recv_sem=s_dh.at[f - 1, p, q],
                    device_id=dev(dy=f, zl_at=p), device_id_type=pl.DeviceIdType.MESH,
                ).wait_recv()
    dhp.wait_recv()

    HO, HW = (0, 256, 512, 768), (256, 256, 256, 128)
    def sum_dh(t):
        cols = pl.ds(HO[t], HW[t])
        v = dh_s[zl, y, :, cols].astype(F32) + dh_p[:, cols].astype(F32)
        for f in range(3):
            v = v + (dh_r[f, 0, :, cols].astype(F32) + dh_r[f, 1, :, cols].astype(F32))
        dhf[y, zl, :, cols] = v.astype(BF)

    sum_dh(3)
    own = dhf.at[y, zl, :, pl.ds(HO[3], HW[3])]
    first = [
        send(own, own, s_go.at[2 * f + g - 1], dev(dy=f, dzl=g))
        for f, g in ((2, 1), (2, 0), (1, 1), (3, 1), (1, 0), (3, 0), (0, 1))
    ]
    for t in range(3):
        sum_dh(t)
    dhg = [Gather(dhf, sems, pl.ds(HO[t], HW[t])) for t, sems in enumerate((s_g0, s_g1, s_g2))]

    gdc.wait_recv()
    gd_o[0:384] = (gd_acc[0:384] + gd_r[0:384].astype(F32)).astype(BF)
    gd_o[384:432] = (
        gd_acc[pl.ds(pl.multiple_of(384 + c * 48, 8), 48)] + gd_r[384:432].astype(F32)
    ).astype(BF)
    ab.finish()
    outs.append(pltpu.make_async_copy(gd_o, gd_ref, s_out.at[1]))
    outs[1].start()

    dwc, dwz, dwl = {}, {}, {}

    def grads_chunk(t):
        if t < 3:
            dhg[t].finish()
        else:
            for cp in first:
                cp.wait_recv()
        cols = pl.ds(CO[t], CW[t])

        def multiply(i, _):
            e, g = i // 2, i % 2
            if t < 3:
                for k in range(2):
                    dh = dhf[e, g, :, t * 256 + k * 128 : t * 256 + k * 128 + 128].astype(F32)
                    for m in range(2):
                        at = pl.ds(CO[t] + k * 256 + m * 128, 128)
                        dgf[e, g, :, at] = (dh * abf[e, g, :, at].astype(F32)).astype(BF)
            else:
                dh = dhf[e, g, :, 768:896].astype(F32)
                for k in range(2):
                    one = jnp.where(lane < 48, dh if k == 0 else pltpu.roll(dh, 80, 1), 0.0)
                    at = pl.ds(CO[3] + k * 128, 128)
                    both = one + pltpu.roll(one, 48, 1)
                    dgf[e, g, :, at] = (both * abf[e, g, :, at].astype(F32)).astype(BF)
            return 0

        lax.fori_loop(0, 8, multiply, 0)

    def dw_chunk(t):
        nc = CW[t] // 2
        for core, buf in ((1 - c, dw_s), (c, dw_acc)):
            v = t_dot(tokf[...].reshape(768, 640), dgf[:, :, :, wide(t, core)].reshape(768, nc))
            buf[:, narrow(t)] = v.astype(buf.dtype)
            if buf is dw_s:
                dwc[t] = send(dw_s.at[:, narrow(t)], dw_r.at[:, narrow(t)], s_dwc.at[t], dev(dc=1))

    def dt_chunk(t):
        cols = pl.ds(CO[t], CW[t])
        for i in range(2):
            w = wf[:, :, cols].reshape(640, CW[t])
            v = dot_t(dgf[2 * i : 2 * i + 2, :, :, cols].reshape(384, CW[t]), w).reshape(2, 192, 640)
            dt_acc[2 * i : 2 * i + 2] = v if t == 3 else dt_acc[2 * i : 2 * i + 2] + v

    def send_dw(t):
        dwc[t].wait_recv()
        at = narrow(t)
        v = (dw_acc[:, at] + dw_r[:, at].astype(F32)).astype(BF)
        dw_o[:, :, at] = v.reshape(4, 160, v.shape[1])
        cp = pltpu.make_async_copy(dw_o.at[zh, :, at], dw_f.at[zh, :, at], s_wl.at[t])
        cp.start()
        dwl[t] = cp
        dwz[t] = [
            send(dw_o.at[flip(zh, e), :, at], dw_f.at[zh, :, at],
                 s_dwz.at[t, e - 1], dev(dzh=e))
            for e in (2, 1, 3)
        ]

    sent(first)
    dhg[0].start_z()
    dhg[0].start()
    grads_chunk(3)
    dw_chunk(3)
    dhg[0].neighbour()
    dhg[1].start_z()
    dhg[1].start()
    dt_chunk(3)
    send_dw(3)
    dhg[0].onward(0)
    dhg[0].onward(1)
    dhg[1].neighbour()
    dhg[2].start_z()
    dhg[2].start()
    grads_chunk(0)
    dw_chunk(0)
    dt_chunk(0)
    dhg[1].onward(0)
    send_dw(0)
    dhg[1].onward(1)
    dhg[2].neighbour()
    grads_chunk(1)
    dw_chunk(1)
    dt_chunk(1)
    dhg[2].onward(0)
    send_dw(1)
    dhg[2].onward(1)
    grads_chunk(2)
    dt_chunk(2)

    def last_dw():
        dw_chunk(2)
        send_dw(2)

    dtv = reduce_tokens(lambda f, e: dt_acc[e], dt_own, dt_s, dt_r, dt2_s, dt2_r, s_dtx, s_dtz, (0, 1, 3, 2), last_dw)
    dt_o[...] = dtv.astype(BF)
    outs.append(pltpu.make_async_copy(dt_o, dtok_ref, s_out.at[2]))
    outs[2].start()
    for t in range(4):
        dwl[t].wait()
        for cp in dwz[t]:
            cp.wait_recv()
    for m, out, to in ((0, gw, dg_ref), (1, uw, du_ref)):
        for n in range(14):
            total = None
            for j in range(4):
                for t in range(4):
                    lo = 432 * j + 128 * t
                    size = 128 if t < 3 else 48
                    if lo + size <= 128 * n or lo >= 128 * n + 128:
                        continue
                    at, off = (t * 256 + m * 128, 0) if t < 3 else (768, 48 * m)
                    v = dw_f[j, :, at : at + 128].astype(F32)
                    r = (lo - 128 * n - off) % 128
                    v = pltpu.roll(v, r, 1) if r else v
                    first, last = max(lo - 128 * n, 0), min(lo + size - 128 * n, 128)
                    keep = (lane160 >= first) & (lane160 < last)
                    total = jnp.where(keep, v, 0.0 if total is None else total)
            total = total.astype(BF)
            if n < 13:
                out[:, 128 * n : 128 * n + 128] = total
            else:
                out[:, 1664:1728] = total[:, 0:64]
        outs.append(pltpu.make_async_copy(out, to, s_out.at[3 + m]))
        outs[3 + m].start()
    for cp in outs:
        cp.wait()
    for cp in pending.values():
        cp.wait_send()


def hand_over(*refs):
    for k in range(5):
        refs[5 + k][...] = refs[k][...]


def body(tokens, gate_weight, up_weight, down_weight, cotangent, penalty_weight):
    V, D = pltpu.VMEM, pltpu.SemaphoreType.DMA
    scratch = [
        V((160, 1728), BF), V((160, 1728), BF), V((48, 640), BF), V((48, 640), BF), V((432, 640), BF), V((4, 160, 896), BF),
        V((4, 160, 1792), BF), V((4, 4, 48, 640), BF), V((192, 1792), BF), V((2, 96, 1792), BF), V((2, 192, 1792), F32),
        V((2, 192, 1792), BF), V((2, 192, 1792), BF),
        V((192, 1792), F32), V((96, 1792), F32), V((96, 1792), BF), V((96, 1792), BF),
        V((4, 2, 96, 1792), BF), V((4, 2, 96, 896), BF), V((896, 640), BF),
        V((4, 48, 640), F32), V((4, 3, 48, 640), BF), V((3, 4, 48, 640), BF), V((3, 48, 640), BF), V((3, 48, 640), BF),
        V((3, 8, 640), F32), V((10, 8, 640), F32), V((4, 4, 48, 640), BF), V((4, 4, 48, 640), BF), V((4, 4, 48, 640), BF),
        V((2, 4, 96, 896), BF), V((3, 2, 96, 896), BF), V((96, 896), BF),
        V((512, 640), F32), V((432, 640), BF), V((432, 640), BF), V((4, 2, 96, 896), BF),
        V((4, 2, 96, 1792), BF), V((4, 192, 640), F32),
        V((4, 48, 640), F32), V((4, 3, 48, 640), BF), V((3, 4, 48, 640), BF), V((3, 48, 640), BF), V((3, 48, 640), BF),
        V((640, 896), F32), V((640, 896), BF), V((640, 896), BF), V((4, 160, 896), BF), V((4, 160, 896), BF),
        D((SLOTS,)), D((4,)), D((5,)), D((3,)), D((12,)), D((4, 3)), D((4,)), D((4,)), D((4, 2)), D((4, 2)), D((4,)), D((9,)),
        D((4,)), D((4,)), D((4, 3)), D((3,)), D((10,)),
        D((3,)), D((12,)), D((3,)), D((3,)), D((9,)),
        D((3, 2, 2)), D((1,)), D((1,)), D((7,)), D((9,)), D((9,)), D((9,)),
        D((4, 3)), D((3,)), D((4,)), D((4, 3)),
    ]
    S = jax.ShapeDtypeStruct
    in_vmem = pl.BlockSpec(memory_space=pltpu.VMEM)
    in_any = pl.BlockSpec(memory_space=pl.ANY)
    shapes = [S((48, 640), BF), S((48, 640), BF), S((160, 1728), BF), S((160, 1728), BF), S((432, 640), BF)]
    results = pl.pallas_call(
        kernel,
        out_shape=shapes,
        in_specs=[in_any] * 5 + [in_vmem],
        out_specs=[in_any] * 5,
        scratch_shapes=scratch,
        compiler_params=pltpu.CompilerParams(
            collective_id=0, has_side_effects=True, vmem_limit_bytes=58 * 2**20
        ),
        cost_estimate=pl.CostEstimate(flops=8 * 10**9, bytes_accessed=6 * 10**6, transcendentals=0),
        name="ffn",
    )(gate_weight, up_weight, tokens, down_weight, cotangent, penalty_weight)
    return tuple(
        pl.pallas_call(
            hand_over,
            out_shape=shapes,
            in_specs=[in_vmem] * 5,
            out_specs=[in_vmem] * 5,
            name="hand_over",
        )(*results)
    )


def solution(mesh):
    in_specs = (
        P(("gy", "gx"), "gz"),
        P(("gz", "gy"), "gx"),
        P(("gz", "gy"), "gx"),
        P(("gx", "gy"), "gz"),
        P(("gy", "gx"), "gz"),
        P("gz"),
    )
    out_specs = (
        P(("gy", "gx"), "gz"),
        P(("gy", "gx"), "gz"),
        P(("gz", "gy"), "gx"),
        P(("gz", "gy"), "gx"),
        P(("gx", "gy"), "gz"),
    )
    return jax.shard_map(body, mesh=mesh, in_specs=in_specs, out_specs=out_specs, check_vma=False)
```

time: 229 us -> 182 us (0.79); the launches traced: 226 us -> 182 us
  Pallas kernels: 212 us -> 181 us
  local copies, waits for them, and re-layouts: 12.2 us -> 0 us
    pallas_call x1 -> x2, Pallas kernels: 212 us -> 181 us  [the longest x1 178 us: body(): pl.pallas_call(kernel, out_shape=shapes, in_specs=[in_any] * 5 + [in_vmem...]
    squeeze x3 -> x0, local copies, waits for them, and re-layouts: 3.21 us -> none  [the longest x2 2.08 us: assemble(): dw[j, :, 256 * t + 128 * first:256 * t + 128 * first + 128]]
    concatenate x6 -> x0, local copies, waits for them, and re-layouts: 2.81 us -> none  [the longest x2 2.29 us: assemble(): return jnp.concatenate(parts, 1)]
    slice x3 -> x0, local copies, waits for them, and re-layouts: 2.77 us -> none  [the longest x2 1.59 us: body(): parts += [g[:, 128 * t:128 * t + 128], u[:, 128 * t:128 * t + 128]]]
where the time goes in v2:
time: 182 us
  Pallas kernels  181 us (99%)
    pallas_call x1, Pallas kernels, body(): pl.pallas_call(kernel, out_shape=shapes, in_specs=[in_any] * 5 + [in_vmem...  178 us

profile of v2, /device:TPU:1, one launch (start us, length us, event | category | flops | bytes accessed | tf_op | source)
XLA Modules:
  0.0 181.7 jit_solution(15718156651591527962)
XLA Ops:
  0.6 178.4 %ffn.1 = (bf16[48,640]{1,0:T(8,128)(2,1)}, bf16[48,640]{1,0:T(8,128)(2,1)}, bf16[160,1728]{1,0:T(8,128)(2,1)}, bf16[160,1728]{1,0:T(8,128)(2,1)}, bf16[432,640]{1,0:T(8,128)(2,1)}) custom-call(bf16[160,1728]{1,0:T(8,128)(2,1)} %gw_ref.1, bf16[160,1728]{1,0:T(8,128)(2,1)} %uw_ref.1, bf16[48,640]{1,0:T(8,128)(2,1)} %tok_ref.1, bf16[432,640]{1,0:T(8,128)(2,1)} %wd_ref.1, ...), custom_call_target="tpu_custom_call" | custom-call | flops 8000000000 | bytes 6000000 | tf_op jit(solution)/shard_map/ffn/pallas_call | solution.py:638
  179.0 2.7 %hand_over.1 = (bf16[48,640]{1,0:T(8,128)(2,1)}, bf16[48,640]{1,0:T(8,128)(2,1)}, bf16[160,1728]{1,0:T(8,128)(2,1)}, bf16[160,1728]{1,0:T(8,128)(2,1)}, bf16[432,640]{1,0:T(8,128)(2,1)}) custom-call(bf16[48,640]{1,0:T(8,128)(2,1)} %get-tuple-element.10.refs_0_, bf16[48,640]{1,0:T(8,128)(2,1)} %get-tuple-element.11.refs_1_, ...), custom_call_target="tpu_custom_call" | custom-call | tf_op jit(solution)/shard_map/hand_over/pallas_call | solution.py:651

commit v3 on v2

--- a/solution.py
+++ b/solution.py
@@ -10,7 +10,7 @@
 NT = 1536.0
 CO = (0, 512, 1024, 1536)
 CW = (512, 512, 512, 256)
-SLOTS = 64
+SLOTS = 48
 
 
 def dot(a, b):
@@ -61,7 +61,7 @@
     abf, hidf, wdf, y_own, y_s, y_r, y2_s, y2_r, mom, mom_r, mxf, cotf, gyf,
     dh_s, dh_r, dh_p, gd_acc, gd_s, gd_r, dhf,
     dgf, dt_acc, dt_own, dt_s, dt_r, dt2_s, dt2_r, dw_acc, dw_s, dw_r, dw_o, dw_f,
-    s_send, s_in, s_out, s_tz, s_tx, s_wz, s_wl, s_wc, s_ph, s_py, s_pz, s_h, s_wd, s_wdl, s_yx, s_yz, s_m,
+    s_send, s_in, s_out, s_tz, s_tx, s_wz, s_wl, s_wc, s_ph, s_py, s_pz, s_h, s_h2, s_wd, s_wdl, s_yx, s_yz, s_ys, s_m,
     s_gz, s_gx, s_cz, s_cx, s_ab, s_dh, s_dhp, s_gd, s_go, s_g0, s_g1, s_g2, s_dtx, s_dtz, s_dwc, s_dwz,
 ):
     gx, gy, gz = lax.axis_index("gx"), lax.axis_index("gy"), lax.axis_index("gz")
@@ -95,6 +95,12 @@
         cp.start()
         pending[slot] = cp
         return cp
+
+    def arrive(ref, sem):
+        pltpu.make_async_remote_copy(
+            src_ref=ref, dst_ref=ref, send_sem=s_send.at[0], recv_sem=sem,
+            device_id=dev(dc=1), device_id_type=pl.DeviceIdType.MESH,
+        ).wait_recv()
 
     def sent(cps):
         for slot in [k for k, cp in pending.items() if any(cp is other for other in cps)]:
@@ -136,6 +142,36 @@
     stage(0)
     pl.semaphore_wait(barrier, len(peers))
 
+    class Gather:
+        def __init__(self, ref, sems, cols):
+            self.ref, self.sems, self.cols, self.cps = ref, sems, cols, {}
+
+        def go(self, k, a, b, to, rows=pl.ds(0, 96)):
+            block = self.ref.at[a, b, rows, self.cols]
+            self.cps[k] = send(block, block, self.sems.at[k], to)
+
+        def start_z(self):
+            self.go(0, y, zl, dev(dzl=1))
+
+        def start(self):
+            for k in range(2):
+                self.go(1 + k, y, zl, dev(dy=1 + 2 * k))
+
+        def neighbour(self):
+            self.cps[0].wait_recv()
+            for k in range(2):
+                self.go(3 + k, y, 1 - zl, dev(dy=1 + 2 * k))
+
+        def onward(self, g):
+            for k in range(2):
+                self.cps[1 + 2 * g + k].wait_recv()
+                z = 1 - zl if g else zl
+                self.go(5 + 2 * g + k, flip(y, 1 + 2 * k), z, dev(dy=3 - 2 * k), pl.ds(48 * k, 48))
+
+        def finish(self):
+            for k in range(5, 9):
+                self.cps[k].wait_recv()
+
     tz = [send(tokf.at[0, 0], tokf.at[e, 0], s_tz.at[e - 1], dev(dzh=e)) for e in (1, 3, 2)]
     wz, wl, wc = [], [], []
 
@@ -145,24 +181,25 @@
         wl.append(cp)
         wz.append([
             send(s_ref.at[flip(zh, e), :, narrow(t)], wf.at[zh, :, wide(t, c)],
-                 s_wz.at[t, e - 1], dev(dzh=e))
+                 s_wz.at[t], dev(dzh=e))
             for e in (2, 1, 3)
         ])
 
     def forward_w(t):
         wl[t].wait()
-        for cp in wz[t]:
-            cp.wait_recv()
+        arrive(wf.at[0:3, :, wide(t, c)], s_wz.at[t])
         wc.append(send(wf.at[:, :, wide(t, c)], wf.at[:, :, wide(t, c)], s_wc.at[t], dev(dc=1)))
 
-    tx = [send(tokf.at[0, 0], tokf.at[0, d], s_tx.at[d - 1], dev(dx=d)) for d in (2, 1, 3)]
+    for d in (2, 1, 3):
+        send(tokf.at[0, 0], tokf.at[0, d], s_tx.at[0], dev(dx=d))
     stage(1)
     sent(tz)
     issue_w(0)
     stage(2)
     for e, cp in zip((1, 3, 2), tz):
         cp.wait_recv()
-        tx += [send(tokf.at[e, 0], tokf.at[e, d], s_tx.at[3 * e + d - 1], dev(dx=d)) for d in (2, 1, 3)]
+        for d in (2, 1, 3):
+            send(tokf.at[e, 0], tokf.at[e, d], s_tx.at[0], dev(dx=d))
     stage(3)
     wdl, wdr = [], []
     for t in range(4):
@@ -176,9 +213,7 @@
         wdr.append(send(wd_ref.at[src], wdf.at[at], s_wd.at[t], dev(dc=1)))
     wdf[864:896, :] = jnp.zeros((32, 640), BF)
 
-    py, pz = [], []
-
-    halves = []
+    pz = []
 
     def matmul_pre(t):
         wc[t].wait_recv()
@@ -188,33 +223,26 @@
             v = dot(tokf[flip(y, f)].reshape(192, 640), w)
             if f == 2:
                 pre_h[:, cols] = v.astype(BF)
-                halves.append([
-                    send(pre_h.at[96 * k : 96 * k + 96, cols], pre_hr.at[k, :, cols], s_ph.at[t, k],
-                         dev(dy=1 + 2 * k))
-                    for k in range(2)
-                ])
+                for k in range(2):
+                    send(pre_h.at[96 * k : 96 * k + 96, cols], pre_hr.at[k, :, cols], s_ph.at[t], dev(dy=1 + 2 * k))
             elif f:
                 pre_f[f // 2, :, cols] = v
             else:
                 pre_own[:, cols] = v
 
     def relay(t):
-        for cp in halves[t]:
-            cp.wait_recv()
         cols = pl.ds(CO[t], CW[t])
+        arrive(pre_hr.at[:, :, cols], s_ph.at[t])
         pre_s[0, 0:96, cols] = pre_f[0, 0:96, cols].astype(BF)
         pre_s[0, 96:192, cols] = (pre_f[0, 96:192, cols] + pre_hr[1, :, cols].astype(F32)).astype(BF)
         pre_s[1, 0:96, cols] = (pre_f[1, 0:96, cols] + pre_hr[0, :, cols].astype(F32)).astype(BF)
         pre_s[1, 96:192, cols] = pre_f[1, 96:192, cols].astype(BF)
-        py.append([
-            send(pre_s.at[k, :, cols], pre_r.at[k, :, cols], s_py.at[t, k], dev(dy=1 + 2 * k))
-            for k in range(2)
-        ])
+        for k in range(2):
+            send(pre_s.at[k, :, cols], pre_r.at[k, :, cols], s_py.at[t], dev(dy=1 + 2 * k))
 
     def sum_y(t):
-        for cp in py[t]:
-            cp.wait_recv()
         cols = pl.ds(CO[t], CW[t])
+        arrive(pre_r.at[:, :, cols], s_py.at[t])
 
         def half(h):
             rows = pl.ds(pl.multiple_of(h * 96, 16), 96)
@@ -259,8 +287,7 @@
     sent(wz[0])
     issue_w(1)
     forward_w(0)
-    for cp in tx:
-        cp.wait_recv()
+    arrive(tokf.at[0:3], s_tx.at[0])
     matmul_pre(0)
     sent(wz[1])
     issue_w(2)
@@ -270,157 +297,149 @@
     sent(wz[2])
     issue_w(3)
     forward_w(2)
-    cz = [send(cotf.at[0, 0], cotf.at[e, 0], s_cz.at[e - 1], dev(dzh=e)) for e in (2, 1, 3)]
     matmul_pre(2)
     relay(1)
     sum_y(0)
     forward_w(3)
+    for e in (2, 1, 3):
+        send(cotf.at[0, 0], cotf.at[e, 0], s_cz.at[0], dev(dzh=e))
+    matmul_pre(3)
     relay(2)
-    matmul_pre(3)
     sum_y(1)
     relay(3)
     finish_pre(0)
     sum_y(2)
-    for cp in cz:
-        cp.wait_recv()
-    cxs = [send(cotf.at[:, 0], cotf.at[:, d], s_cx.at[d - 1], dev(dx=d)) for d in (2, 1, 3)]
+    arrive(cotf.at[0:3, 0], s_cz.at[0])
+    for d in (2, 1, 3):
+        send(cotf.at[:, 0], cotf.at[:, d], s_cx.at[0], dev(dx=d))
+    finish_pre(1)
+    hid = [Gather(hidf, s_h, pl.ds(0, 512)), Gather(hidf, s_h2, pl.ds(512, 384))]
+    hid[0].start_z()
     sum_y(3)
-    finish_pre(1)
+    hid[0].start()
     finish_pre(2)
     finish_pre(3)
 
-    class Gather:
-        def __init__(self, ref, sems, cols):
-            self.ref, self.sems, self.cols, self.cps = ref, sems, cols, {}
-
-        def go(self, k, a, b, to, rows=pl.ds(0, 96)):
-            block = self.ref.at[a, b, rows, self.cols]
-            self.cps[k] = send(block, block, self.sems.at[k], to)
-
-        def start_z(self):
-            self.go(0, y, zl, dev(dzl=1))
-
-        def start(self):
-            for k in range(2):
-                self.go(1 + k, y, zl, dev(dy=1 + 2 * k))
-
-        def neighbour(self):
-            self.cps[0].wait_recv()
-            for k in range(2):
-                self.go(3 + k, y, 1 - zl, dev(dy=1 + 2 * k))
-
-        def onward(self, g):
-            for k in range(2):
-                self.cps[1 + 2 * g + k].wait_recv()
-                z = 1 - zl if g else zl
-                self.go(5 + 2 * g + k, flip(y, 1 + 2 * k), z, dev(dy=3 - 2 * k), pl.ds(48 * k, 48))
-
-        def finish(self):
-            for k in range(5, 9):
-                self.cps[k].wait_recv()
-
-    hid = Gather(hidf, s_h, pl.ds(0, 896))
-    hid.start_z()
-    hid.start()
+    hid[1].start_z()
+    hid[1].start()
+    hid[0].neighbour()
     for cp in wdl:
         cp.wait()
     for cp in wdr:
         cp.wait_recv()
-    hid.neighbour()
+    hid[0].onward(0)
+    hid[1].neighbour()
     ab = Gather(abf, s_ab, pl.ds(0, 1792))
     ab.start_z()
 
-    def reduce_tokens(make_rows, own_buf, s_buf, r_buf, s2_buf, r2_buf, sem_x, sem_z, order, between=None):
-        xs = []
-        for k, f in enumerate(order):
-            e = flip(y, f)
-            v = make_rows(f, e).reshape(4, 48, 640)
-            own_buf[e] = v[0]
-            s_buf[e] = v[1:4].astype(BF)
-            for d in (2, 1, 3):
-                xs.append(send(s_buf.at[e, d - 1], r_buf.at[d - 1, e], sem_x.at[k, d - 1], dev(dx=d)))
-        if between is not None:
-            between()
-        for cp in xs:
-            cp.wait_recv()
-        zs = []
-
-        def total(e):
-            return (own_buf[e] + r_buf[0, e].astype(F32)) + (
-                r_buf[1, e].astype(F32) + r_buf[2, e].astype(F32)
-            )
-
-        for e in (2, 1, 3):
-            s2_buf[e - 1] = total(e).astype(BF)
-            zs.append(send(s2_buf.at[e - 1], r2_buf.at[e - 1], sem_z.at[e - 1], dev(dzh=e)))
-        own = total(0)
-        for cp in zs:
-            cp.wait_recv()
-        return (own + r2_buf[0].astype(F32)) + (r2_buf[1].astype(F32) + r2_buf[2].astype(F32))
+    def split_x(k, e, v, own_buf, s_buf, r_buf, sem):
+        v = v.reshape(4, 48, 640)
+        own_buf[e] = v[0]
+        s_buf[e] = v[1:4].astype(BF)
+        for d in (2, 1, 3):
+            send(s_buf.at[e, d - 1], r_buf.at[d - 1, e], sem.at[k], dev(dx=d))
+
+    def total_x(e, own_buf, r_buf):
+        return (own_buf[e] + r_buf[0, e].astype(F32)) + (r_buf[1, e].astype(F32) + r_buf[2, e].astype(F32))
 
     def y_rows(f, e):
         if f == 1:
-            hid.onward(0)
-            hid.onward(1)
+            hid[0].onward(1)
+            hid[1].onward(0)
+            hid[1].onward(1)
         elif f == 2:
-            hid.finish()
+            hid[0].finish()
+            hid[1].finish()
         return dot(hidf[e].reshape(192, 896), wdf[...])
 
     def after_y():
         ab.start()
         ab.neighbour()
 
-    yv = reduce_tokens(y_rows, y_own, y_s, y_r, y2_s, y2_r, s_yx, s_yz, (0, 1, 3, 2), after_y)
+    for k, f in enumerate((0, 1, 3, 2)):
+        e = flip(y, f)
+        split_x(k, e, y_rows(f, e), y_own, y_s, y_r, s_yx)
+    after_y()
+    def to_owner(k, e):
+        other = ((zh // 2 + e // 2) % 2) * 2 + (zh % 2 + e % 2) % 2
+        return pltpu.make_async_remote_copy(
+            src_ref=y2_s.at[k], dst_ref=y2_r.at[lax.max(e, 1) - 1], send_sem=s_ys.at[k], recv_sem=s_yz.at[0],
+            device_id=(gx, other, gz), device_id_type=pl.DeviceIdType.MESH,
+        )
+
+    for k, f in enumerate((0, 1, 3, 2)):
+        e = flip(y, f)
+        arrive(y_r.at[:, e], s_yx.at[k])
+        v = total_x(e, y_own, y_r)
+        y2_s[k] = (v * v * v).astype(BF)
+
+        @pl.when(e != 0)
+        def _(k=k, e=e):
+            to_owner(k, e).start()
+
+    yv = total_x(0, y_own, y_r)
+    arrive(y2_r, s_yz.at[0])
+    for e in range(3):
+        yv = yv + cube_root(y2_r[e].astype(F32))
 
     sq = yv * yv
     mom[0, 0:4] = jnp.concatenate(
         [jnp.sum(v, 0, keepdims=True) for v in (yv, sq, sq * yv, sq * sq)], 0
     )
     mom[0, 4:8] = jnp.zeros((4, 640), F32)
-    cps = [
-        send(mom.at[0], mom_r.at[2 * d + k - 1], s_m.at[2 * d + k - 1], dev(dx=d, dc=k))
-        for d in (2, 1, 3, 0) for k in (1, 0) if (d, k) != (0, 0)
-    ]
+    for d in (2, 1, 3, 0):
+        for k in (1, 0):
+            if (d, k) != (0, 0):
+                send(mom.at[0], mom_r.at[2 * d + k - 1], s_m.at[0], dev(dx=d, dc=k))
     mxf[0, 0] = (sq * yv).astype(BF)
     mz = [send(mxf.at[0, 0], mxf.at[e, 0], s_gz.at[e - 1], dev(dzh=e)) for e in (1, 3, 2)]
-    mx = {d: [send(mxf.at[0, 0], mxf.at[0, d], s_gx.at[d - 1], dev(dx=d))] for d in (2, 1, 3)}
+    for d in (2, 1, 3):
+        send(mxf.at[0, 0], mxf.at[0, d], s_gx.at[d], dev(dx=d))
     mix[...] = yv.astype(BF)
     outs = [pltpu.make_async_copy(mix, mixed_ref, s_out.at[0])]
     outs[0].start()
-    for cp in cps:
-        cp.wait_recv()
+    arrive(mom_r.at[0:7], s_m.at[0])
     mom[1] = ((mom[0] + mom_r[0]) + (mom_r[1] + mom_r[2])) + ((mom_r[3] + mom_r[4]) + (mom_r[5] + mom_r[6]))
-    ms = [send(mom.at[1], mom_r.at[6 + e], s_m.at[6 + e], dev(dzh=e)) for e in (2, 1, 3)]
+    for e in (2, 1, 3):
+        send(mom.at[1], mom_r.at[6 + e], s_m.at[1], dev(dzh=e))
     for e, cp in zip((1, 3, 2), mz):
         cp.wait_recv()
         for d in (2, 1, 3):
-            mx[d].append(send(mxf.at[e, 0], mxf.at[e, d], s_gx.at[3 * e + d - 1], dev(dx=d)))
+            send(mxf.at[e, 0], mxf.at[e, d], s_gx.at[d], dev(dx=d))
     ab.onward(0)
     ab.onward(1)
-    for cp in ms:
-        cp.wait_recv()
+    arrive(mom_r.at[7:10], s_m.at[1])
     mom[2] = (mom[1] + mom_r[7]) + (mom_r[8] + mom_r[9])
-    for cp in cxs:
-        cp.wait_recv()
+    arrive(cotf.at[:, 1:4], s_cx.at[0])
 
     def dh_rows(d):
         if d:
-            for cp in mx[d]:
-                cp.wait_recv()
+            arrive(mxf.at[:, d], s_gx.at[d])
         totals, weight = mom[2], pw_ref[...].reshape(1, 640)
         for e in range(4):
             gyf[e, d] = penalty_grad(cube_root(mxf[e, d].astype(F32)), totals, cotf[e, d], weight)
         v = dot_t(gyf[:, d].reshape(192, 640), wdf[...])
         dh_s[d // 2, :, (d % 2) * 48 : (d % 2) * 48 + 48, :] = v.astype(BF).reshape(4, 48, 896)
 
-    for d in (0, 1, 3, 2):
-        dh_rows(d)
+    PART = (pl.ds(512, 384), pl.ds(0, 512))
+
+    def send_rows(d, part):
         p, q = d // 2, d % 2
         rows = pl.ds(48 * q, 48)
         for f in (2, 1, 3):
-            send(dh_s.at[p, flip(y, f), rows], dh_r.at[f - 1, zl, rows],
-                 s_dh.at[f - 1, zl, q], dev(dy=f, zl_at=p))
-    dhp = send(dh_s.at[1 - zl, y], dh_p, s_dhp.at[0], dev(dzl=1))
+            send(dh_s.at[p, flip(y, f), rows, PART[part]], dh_r.at[f - 1, zl, rows, PART[part]],
+                 s_dh.at[part], dev(dy=f, zl_at=p))
+
+    for d in (0, 1, 3, 2):
+        dh_rows(d)
+        send_rows(d, 0)
+        if d == 0:
+            send_rows(0, 1)
+    for part in range(2):
+        if part:
+            for d in (1, 3, 2):
+                send_rows(d, 1)
+        send(dh_s.at[1 - zl, y, :, PART[part]], dh_p.at[:, PART[part]], s_dhp.at[part], dev(dzl=1))
 
     def gd_part(core, t):
         if t < 3:
@@ -437,17 +456,6 @@
     for t in range(3):
         gd_acc[t * 128 : t * 128 + 128] = gd_part(c, t)
 
-    for f in (1, 2, 3):
-        for p in range(2):
-            for q in range(2):
-                rows = pl.ds(48 * q, 48)
-                pltpu.make_async_remote_copy(
-                    src_ref=dh_s.at[p, flip(y, f), rows], dst_ref=dh_r.at[f - 1, p, rows],
-                    send_sem=s_send.at[0], recv_sem=s_dh.at[f - 1, p, q],
-                    device_id=dev(dy=f, zl_at=p), device_id_type=pl.DeviceIdType.MESH,
-                ).wait_recv()
-    dhp.wait_recv()
-
     HO, HW = (0, 256, 512, 768), (256, 256, 256, 128)
     def sum_dh(t):
         cols = pl.ds(HO[t], HW[t])
@@ -456,15 +464,24 @@
             v = v + (dh_r[f, 0, :, cols].astype(F32) + dh_r[f, 1, :, cols].astype(F32))
         dhf[y, zl, :, cols] = v.astype(BF)
 
-    sum_dh(3)
-    own = dhf.at[y, zl, :, pl.ds(HO[3], HW[3])]
-    first = [
-        send(own, own, s_go.at[2 * f + g - 1], dev(dy=f, dzl=g))
-        for f, g in ((2, 1), (2, 0), (1, 1), (3, 1), (1, 0), (3, 0), (0, 1))
-    ]
-    for t in range(3):
+    def dh_arrived(part):
+        arrive(dh_r.at[:, :, :, PART[part]], s_dh.at[part])
+        arrive(dh_p.at[:, PART[part]], s_dhp.at[part])
+
+    direct = {}
+
+    def send_dh(t, sems):
         sum_dh(t)
-    dhg = [Gather(dhf, sems, pl.ds(HO[t], HW[t])) for t, sems in enumerate((s_g0, s_g1, s_g2))]
+        own = dhf.at[y, zl, :, pl.ds(HO[t], HW[t])]
+        direct[t] = [
+            send(own, own, sems.at[2 * f + g - 1], dev(dy=f, dzl=g))
+            for f, g in ((2, 1), (2, 0), (1, 1), (3, 1), (1, 0), (3, 0), (0, 1))
+        ]
+
+    dh_arrived(0)
+    send_dh(3, s_go)
+    send_dh(2, s_g2)
+    dhg = [Gather(dhf, sems, pl.ds(HO[t], HW[t])) for t, sems in enumerate((s_g0, s_g1))]
 
     gdc.wait_recv()
     gd_o[0:384] = (gd_acc[0:384] + gd_r[0:384].astype(F32)).astype(BF)
@@ -475,13 +492,13 @@
     outs.append(pltpu.make_async_copy(gd_o, gd_ref, s_out.at[1]))
     outs[1].start()
 
-    dwc, dwz, dwl = {}, {}, {}
+    dwc, dwl = {}, {}
 
     def grads_chunk(t):
-        if t < 3:
+        if t < 2:
             dhg[t].finish()
         else:
-            for cp in first:
+            for cp in direct[t]:
                 cp.wait_recv()
         cols = pl.ds(CO[t], CW[t])
 
@@ -527,55 +544,50 @@
         cp = pltpu.make_async_copy(dw_o.at[zh, :, at], dw_f.at[zh, :, at], s_wl.at[t])
         cp.start()
         dwl[t] = cp
-        dwz[t] = [
-            send(dw_o.at[flip(zh, e), :, at], dw_f.at[zh, :, at],
-                 s_dwz.at[t, e - 1], dev(dzh=e))
-            for e in (2, 1, 3)
-        ]
-
-    sent(first)
-    dhg[0].start_z()
-    dhg[0].start()
+        for e in (2, 1, 3):
+            send(dw_o.at[flip(zh, e), :, at], dw_f.at[zh, :, at], s_dwz.at[t], dev(dzh=e))
+
     grads_chunk(3)
     dw_chunk(3)
-    dhg[0].neighbour()
-    dhg[1].start_z()
-    dhg[1].start()
+    dh_arrived(1)
+    for t in range(2):
+        sum_dh(t)
+        dhg[t].start_z()
+        dhg[t].start()
     dt_chunk(3)
     send_dw(3)
+    grads_chunk(2)
+    dw_chunk(2)
+    dhg[0].neighbour()
+    dt_chunk(2)
+    send_dw(2)
     dhg[0].onward(0)
+    dhg[1].neighbour()
     dhg[0].onward(1)
-    dhg[1].neighbour()
-    dhg[2].start_z()
-    dhg[2].start()
+    dhg[1].onward(0)
+    dhg[1].onward(1)
     grads_chunk(0)
     dw_chunk(0)
     dt_chunk(0)
-    dhg[1].onward(0)
     send_dw(0)
-    dhg[1].onward(1)
-    dhg[2].neighbour()
     grads_chunk(1)
+    dt_chunk(1)
+
+    for k, e in enumerate((2, 1, 3, 0)):
+        split_x(k, e, dt_acc[e], dt_own, dt_s, dt_r, s_dtx)
     dw_chunk(1)
-    dt_chunk(1)
-    dhg[2].onward(0)
     send_dw(1)
-    dhg[2].onward(1)
-    grads_chunk(2)
-    dt_chunk(2)
-
-    def last_dw():
-        dw_chunk(2)
-        send_dw(2)
-
-    dtv = reduce_tokens(lambda f, e: dt_acc[e], dt_own, dt_s, dt_r, dt2_s, dt2_r, s_dtx, s_dtz, (0, 1, 3, 2), last_dw)
-    dt_o[...] = dtv.astype(BF)
-    outs.append(pltpu.make_async_copy(dt_o, dtok_ref, s_out.at[2]))
-    outs[2].start()
-    for t in range(4):
+    for k, e in enumerate((2, 1, 3, 0)):
+        arrive(dt_r.at[:, e], s_dtx.at[k])
+        v = total_x(e, dt_own, dt_r)
+        if e:
+            dt2_s[e - 1] = v.astype(BF)
+            send(dt2_s.at[e - 1], dt2_r.at[e - 1], s_dtz.at[0], dev(dzh=e))
+        else:
+            dt_own[0] = v
+    for t in (3, 2, 0, 1):
         dwl[t].wait()
-        for cp in dwz[t]:
-            cp.wait_recv()
+        arrive(dw_f.at[0:3, :, narrow(t)], s_dwz.at[t])
     for m, out, to in ((0, gw, dg_ref), (1, uw, du_ref)):
         for n in range(14):
             total = None
@@ -598,16 +610,34 @@
             else:
                 out[:, 1664:1728] = total[:, 0:64]
         outs.append(pltpu.make_async_copy(out, to, s_out.at[3 + m]))
-        outs[3 + m].start()
+        outs[-1].start()
+    arrive(dt2_r, s_dtz.at[0])
+    dt_o[...] = ((dt_own[0] + dt2_r[0].astype(F32)) + (dt2_r[1].astype(F32) + dt2_r[2].astype(F32))).astype(BF)
+    outs.append(pltpu.make_async_copy(dt_o, dtok_ref, s_out.at[2]))
+    outs[-1].start()
     for cp in outs:
         cp.wait()
+    for k, f in enumerate((0, 1, 3, 2)):
+        e = flip(y, f)
+
+        @pl.when(e != 0)
+        def _(k=k, e=e):
+            to_owner(k, e).wait_send()
+
     for cp in pending.values():
         cp.wait_send()
 
 
 def hand_over(*refs):
+    ins = [pltpu.make_async_copy(refs[k], refs[10 + k], refs[15].at[k]) for k in range(5)]
+    outs = [pltpu.make_async_copy(refs[10 + k], refs[5 + k], refs[16].at[k]) for k in range(5)]
+    for cp in ins:
+        cp.start()
     for k in range(5):
-        refs[5 + k][...] = refs[k][...]
+        ins[k].wait()
+        outs[k].start()
+    for cp in outs:
+        cp.wait()
 
 
 def body(tokens, gate_weight, up_weight, down_weight, cotangent, penalty_weight):
@@ -618,18 +648,18 @@
         V((2, 192, 1792), BF), V((2, 192, 1792), BF),
         V((192, 1792), F32), V((96, 1792), F32), V((96, 1792), BF), V((96, 1792), BF),
         V((4, 2, 96, 1792), BF), V((4, 2, 96, 896), BF), V((896, 640), BF),
-        V((4, 48, 640), F32), V((4, 3, 48, 640), BF), V((3, 4, 48, 640), BF), V((3, 48, 640), BF), V((3, 48, 640), BF),
+        V((4, 48, 640), F32), V((4, 3, 48, 640), BF), V((3, 4, 48, 640), BF), V((4, 48, 640), BF), V((3, 48, 640), BF),
         V((3, 8, 640), F32), V((10, 8, 640), F32), V((4, 4, 48, 640), BF), V((4, 4, 48, 640), BF), V((4, 4, 48, 640), BF),
         V((2, 4, 96, 896), BF), V((3, 2, 96, 896), BF), V((96, 896), BF),
         V((512, 640), F32), V((432, 640), BF), V((432, 640), BF), V((4, 2, 96, 896), BF),
         V((4, 2, 96, 1792), BF), V((4, 192, 640), F32),
         V((4, 48, 640), F32), V((4, 3, 48, 640), BF), V((3, 4, 48, 640), BF), V((3, 48, 640), BF), V((3, 48, 640), BF),
         V((640, 896), F32), V((640, 896), BF), V((640, 896), BF), V((4, 160, 896), BF), V((4, 160, 896), BF),
-        D((SLOTS,)), D((4,)), D((5,)), D((3,)), D((12,)), D((4, 3)), D((4,)), D((4,)), D((4, 2)), D((4, 2)), D((4,)), D((9,)),
-        D((4,)), D((4,)), D((4, 3)), D((3,)), D((10,)),
-        D((3,)), D((12,)), D((3,)), D((3,)), D((9,)),
-        D((3, 2, 2)), D((1,)), D((1,)), D((7,)), D((9,)), D((9,)), D((9,)),
-        D((4, 3)), D((3,)), D((4,)), D((4, 3)),
+        D((SLOTS,)), D((4,)), D((5,)), D((3,)), D((1,)), D((4,)), D((4,)), D((4,)), D((4,)), D((4,)), D((4,)), D((9,)), D((9,)),
+        D((4,)), D((4,)), D((4,)), D((1,)), D((4,)), D((2,)),
+        D((3,)), D((4,)), D((1,)), D((1,)), D((9,)),
+        D((2,)), D((2,)), D((1,)), D((7,)), D((9,)), D((9,)), D((7,)),
+        D((4,)), D((1,)), D((4,)), D((4,)),
     ]
     S = jax.ShapeDtypeStruct
     in_vmem = pl.BlockSpec(memory_space=pltpu.VMEM)
@@ -651,8 +681,9 @@
         pl.pallas_call(
             hand_over,
             out_shape=shapes,
-            in_specs=[in_vmem] * 5,
-            out_specs=[in_vmem] * 5,
+            in_specs=[in_any] * 5,
+            out_specs=[in_any] * 5,
+            scratch_shapes=[V(a.shape, BF) for a in shapes] + [D((5,)), D((5,))],
             name="hand_over",
         )(*results)
     )

time: 182 us -> 173 us (0.951)
  Pallas kernels: 181 us -> 172 us
    pallas_call x1, Pallas kernels: 178 us -> 170 us  [body(): pl.pallas_call(kernel, out_shape=shapes, in_specs=[in_any] * 5 + [in_vmem...]
where the time goes in v3:
time: 173 us
  Pallas kernels  172 us (99%)
    pallas_call x1, Pallas kernels, body(): pl.pallas_call(kernel, out_shape=shapes, in_specs=[in_any] * 5 + [in_vmem...  170 us

profile of v3, /device:TPU:1, one launch (start us, length us, event | category | flops | bytes accessed | tf_op | source)
XLA Modules:
  0.0 172.8 jit_solution(18063980245423712279)
XLA Ops:
  0.6 169.6 %ffn.1 = (bf16[48,640]{1,0:T(8,128)(2,1)}, bf16[48,640]{1,0:T(8,128)(2,1)}, bf16[160,1728]{1,0:T(8,128)(2,1)}, bf16[160,1728]{1,0:T(8,128)(2,1)}, bf16[432,640]{1,0:T(8,128)(2,1)}) custom-call(bf16[160,1728]{1,0:T(8,128)(2,1)} %gw_ref.1, bf16[160,1728]{1,0:T(8,128)(2,1)} %uw_ref.1, bf16[48,640]{1,0:T(8,128)(2,1)} %tok_ref.1, bf16[432,640]{1,0:T(8,128)(2,1)} %wd_ref.1, ...), custom_call_target="tpu_custom_call" | custom-call | flops 8000000000 | bytes 6000000 | tf_op jit(solution)/shard_map/ffn/pallas_call | solution.py:668
  170.3 2.4 %hand_over.1 = (bf16[48,640]{1,0:T(8,128)(2,1)}, bf16[48,640]{1,0:T(8,128)(2,1)}, bf16[160,1728]{1,0:T(8,128)(2,1)}, bf16[160,1728]{1,0:T(8,128)(2,1)}, bf16[432,640]{1,0:T(8,128)(2,1)}) custom-call(bf16[48,640]{1,0:T(8,128)(2,1)} %get-tuple-element.10.refs_0_, bf16[48,640]{1,0:T(8,128)(2,1)} %get-tuple-element.11.refs_1_, ...), custom_call_target="tpu_custom_call" | custom-call | tf_op jit(solution)/shard_map/hand_over/pallas_call | solution.py:681

commit v4 on v3

--- a/solution.py
+++ b/solution.py
@@ -173,7 +173,7 @@
                 self.cps[k].wait_recv()
 
     tz = [send(tokf.at[0, 0], tokf.at[e, 0], s_tz.at[e - 1], dev(dzh=e)) for e in (1, 3, 2)]
-    wz, wl, wc = [], [], []
+    wz, wl = [], []
 
     def issue_w(t):
         cp = pltpu.make_async_copy(s_ref.at[zh, :, narrow(t)], wf.at[zh, :, wide(t, c)], s_wl.at[t])
@@ -181,14 +181,24 @@
         wl.append(cp)
         wz.append([
             send(s_ref.at[flip(zh, e), :, narrow(t)], wf.at[zh, :, wide(t, c)],
-                 s_wz.at[t], dev(dzh=e))
+                 s_wz.at[t, 1 if e == 2 else 0], dev(dzh=e))
             for e in (2, 1, 3)
         ])
 
     def forward_w(t):
+        cols = wide(t, c)
+
+        def forward(e):
+            piece = wf.at[flip(zh, e), :, cols]
+            send(piece, piece, s_wc.at[t], dev(dc=1))
+
         wl[t].wait()
-        arrive(wf.at[0:3, :, wide(t, c)], s_wz.at[t])
-        wc.append(send(wf.at[:, :, wide(t, c)], wf.at[:, :, wide(t, c)], s_wc.at[t], dev(dc=1)))
+        forward(0)
+        arrive(wf.at[0:2, :, cols], s_wz.at[t, 0])
+        forward(1)
+        forward(3)
+        arrive(wf.at[0, :, cols], s_wz.at[t, 1])
+        forward(2)
 
     for d in (2, 1, 3):
         send(tokf.at[0, 0], tokf.at[0, d], s_tx.at[0], dev(dx=d))
@@ -216,8 +226,8 @@
     pz = []
 
     def matmul_pre(t):
-        wc[t].wait_recv()
         cols = pl.ds(CO[t], CW[t])
+        arrive(wf.at[:, :, wide(t, 1 - c)], s_wc.at[t])
         for f in (2, 1, 3, 0):
             w = wf[:, :, cols].reshape(640, CW[t])
             v = dot(tokf[flip(y, f)].reshape(192, 640), w)
@@ -297,8 +307,8 @@
     sent(wz[2])
     issue_w(3)
     forward_w(2)
+    relay(1)
     matmul_pre(2)
-    relay(1)
     sum_y(0)
     forward_w(3)
     for e in (2, 1, 3):
@@ -329,7 +339,7 @@
         cp.wait_recv()
     hid[0].onward(0)
     hid[1].neighbour()
-    ab = Gather(abf, s_ab, pl.ds(0, 1792))
+    ab = Gather(abf, s_ab, pl.ds(1024, 768))
     ab.start_z()
 
     def split_x(k, e, v, own_buf, s_buf, r_buf, sem):
@@ -398,6 +408,8 @@
     mix[...] = yv.astype(BF)
     outs = [pltpu.make_async_copy(mix, mixed_ref, s_out.at[0])]
     outs[0].start()
+    ab.onward(0)
+    ab.onward(1)
     arrive(mom_r.at[0:7], s_m.at[0])
     mom[1] = ((mom[0] + mom_r[0]) + (mom_r[1] + mom_r[2])) + ((mom_r[3] + mom_r[4]) + (mom_r[5] + mom_r[6]))
     for e in (2, 1, 3):
@@ -406,8 +418,6 @@
         cp.wait_recv()
         for d in (2, 1, 3):
             send(mxf.at[e, 0], mxf.at[e, d], s_gx.at[d], dev(dx=d))
-    ab.onward(0)
-    ab.onward(1)
     arrive(mom_r.at[7:10], s_m.at[1])
     mom[2] = (mom[1] + mom_r[7]) + (mom_r[8] + mom_r[9])
     arrive(cotf.at[:, 1:4], s_cx.at[0])
@@ -457,12 +467,18 @@
         gd_acc[t * 128 : t * 128 + 128] = gd_part(c, t)
 
     HO, HW = (0, 256, 512, 768), (256, 256, 256, 128)
-    def sum_dh(t):
-        cols = pl.ds(HO[t], HW[t])
+    def total_dh(cols):
         v = dh_s[zl, y, :, cols].astype(F32) + dh_p[:, cols].astype(F32)
         for f in range(3):
             v = v + (dh_r[f, 0, :, cols].astype(F32) + dh_r[f, 1, :, cols].astype(F32))
-        dhf[y, zl, :, cols] = v.astype(BF)
+        return v
+
+    def own_grads(t):
+        for k in range(2):
+            dh = total_dh(pl.ds(HO[t] + k * 128, 128))
+            for m in range(2):
+                at = pl.ds(CO[t] + k * 256 + m * 128, 128)
+                dgf[y, zl, :, at] = (dh * abf[y, zl, :, at].astype(F32)).astype(BF)
 
     def dh_arrived(part):
         arrive(dh_r.at[:, :, :, PART[part]], s_dh.at[part])
@@ -471,8 +487,9 @@
     direct = {}
 
     def send_dh(t, sems):
-        sum_dh(t)
-        own = dhf.at[y, zl, :, pl.ds(HO[t], HW[t])]
+        cols = pl.ds(HO[t], HW[t])
+        dhf[y, zl, :, cols] = total_dh(cols).astype(BF)
+        own = dhf.at[y, zl, :, cols]
         direct[t] = [
             send(own, own, sems.at[2 * f + g - 1], dev(dy=f, dzl=g))
             for f, g in ((2, 1), (2, 0), (1, 1), (3, 1), (1, 0), (3, 0), (0, 1))
@@ -481,7 +498,7 @@
     dh_arrived(0)
     send_dh(3, s_go)
     send_dh(2, s_g2)
-    dhg = [Gather(dhf, sems, pl.ds(HO[t], HW[t])) for t, sems in enumerate((s_g0, s_g1))]
+    dhg = [Gather(dgf, sems, pl.ds(CO[t], CW[t])) for t, sems in enumerate((s_g0, s_g1))]
 
     gdc.wait_recv()
     gd_o[0:384] = (gd_acc[0:384] + gd_r[0:384].astype(F32)).astype(BF)
@@ -497,10 +514,9 @@
     def grads_chunk(t):
         if t < 2:
             dhg[t].finish()
-        else:
-            for cp in direct[t]:
-                cp.wait_recv()
-        cols = pl.ds(CO[t], CW[t])
+            return
+        for cp in direct[t]:
+            cp.wait_recv()
 
         def multiply(i, _):
             e, g = i // 2, i % 2
@@ -547,13 +563,13 @@
         for e in (2, 1, 3):
             send(dw_o.at[flip(zh, e), :, at], dw_f.at[zh, :, at], s_dwz.at[t], dev(dzh=e))
 
+    dh_arrived(1)
+    for t in range(2):
+        own_grads(t)
+        dhg[t].start_z()
+        dhg[t].start()
     grads_chunk(3)
     dw_chunk(3)
-    dh_arrived(1)
-    for t in range(2):
-        sum_dh(t)
-        dhg[t].start_z()
-        dhg[t].start()
     dt_chunk(3)
     send_dw(3)
     grads_chunk(2)
@@ -655,7 +671,7 @@
         V((4, 2, 96, 1792), BF), V((4, 192, 640), F32),
         V((4, 48, 640), F32), V((4, 3, 48, 640), BF), V((3, 4, 48, 640), BF), V((3, 48, 640), BF), V((3, 48, 640), BF),
         V((640, 896), F32), V((640, 896), BF), V((640, 896), BF), V((4, 160, 896), BF), V((4, 160, 896), BF),
-        D((SLOTS,)), D((4,)), D((5,)), D((3,)), D((1,)), D((4,)), D((4,)), D((4,)), D((4,)), D((4,)), D((4,)), D((9,)), D((9,)),
+        D((SLOTS,)), D((4,)), D((5,)), D((3,)), D((1,)), D((4, 2)), D((4,)), D((4,)), D((4,)), D((4,)), D((4,)), D((9,)), D((9,)),
         D((4,)), D((4,)), D((4,)), D((1,)), D((4,)), D((2,)),
         D((3,)), D((4,)), D((1,)), D((1,)), D((9,)),
         D((2,)), D((2,)), D((1,)), D((7,)), D((9,)), D((9,)), D((7,)),

time: 173 us -> 172 us (level)
  no operation moved by 1% of the time
where the time goes in v4:
time: 172 us
  Pallas kernels  171 us (99%)
    pallas_call x1, Pallas kernels, body(): pl.pallas_call(kernel, out_shape=shapes, in_specs=[in_any] * 5 + [in_vmem...  168 us

profile of v4, /device:TPU:1, one launch (start us, length us, event | category | flops | bytes accessed | tf_op | source)
XLA Modules:
  0.0 171.6 jit_solution(9836364472549518999)
XLA Ops:
  0.6 168.4 %ffn.1 = (bf16[48,640]{1,0:T(8,128)(2,1)}, bf16[48,640]{1,0:T(8,128)(2,1)}, bf16[160,1728]{1,0:T(8,128)(2,1)}, bf16[160,1728]{1,0:T(8,128)(2,1)}, bf16[432,640]{1,0:T(8,128)(2,1)}) custom-call(bf16[160,1728]{1,0:T(8,128)(2,1)} %gw_ref.1, bf16[160,1728]{1,0:T(8,128)(2,1)} %uw_ref.1, bf16[48,640]{1,0:T(8,128)(2,1)} %tok_ref.1, bf16[432,640]{1,0:T(8,128)(2,1)} %wd_ref.1, ...), custom_call_target="tpu_custom_call" | custom-call | flops 8000000000 | bytes 6000000 | tf_op jit(solution)/shard_map/ffn/pallas_call | solution.py:684
  169.1 2.4 %hand_over.1 = (bf16[48,640]{1,0:T(8,128)(2,1)}, bf16[48,640]{1,0:T(8,128)(2,1)}, bf16[160,1728]{1,0:T(8,128)(2,1)}, bf16[160,1728]{1,0:T(8,128)(2,1)}, bf16[432,640]{1,0:T(8,128)(2,1)}) custom-call(bf16[48,640]{1,0:T(8,128)(2,1)} %get-tuple-element.10.refs_0_, bf16[48,640]{1,0:T(8,128)(2,1)} %get-tuple-element.11.refs_1_, ...), custom_call_target="tpu_custom_call" | custom-call | tf_op jit(solution)/shard_map/hand_over/pallas_call | solution.py:697

commit v5 on v4

--- a/solution.py
+++ b/solution.py
@@ -61,7 +61,7 @@
     abf, hidf, wdf, y_own, y_s, y_r, y2_s, y2_r, mom, mom_r, mxf, cotf, gyf,
     dh_s, dh_r, dh_p, gd_acc, gd_s, gd_r, dhf,
     dgf, dt_acc, dt_own, dt_s, dt_r, dt2_s, dt2_r, dw_acc, dw_s, dw_r, dw_o, dw_f,
-    s_send, s_in, s_out, s_tz, s_tx, s_wz, s_wl, s_wc, s_ph, s_py, s_pz, s_h, s_h2, s_wd, s_wdl, s_yx, s_yz, s_ys, s_m,
+    s_send, s_in, s_out, s_tz, s_tx, s_wz, s_wl, s_wc, s_ph, s_py, s_pz, s_h, s_h2, s_h3, s_wd, s_wdl, s_yx, s_yz, s_ys, s_m,
     s_gz, s_gx, s_cz, s_cx, s_ab, s_dh, s_dhp, s_gd, s_go, s_g0, s_g1, s_g2, s_dtx, s_dtz, s_dwc, s_dwz,
 ):
     gx, gy, gz = lax.axis_index("gx"), lax.axis_index("gy"), lax.axis_index("gz")
@@ -323,22 +323,25 @@
     for d in (2, 1, 3):
         send(cotf.at[:, 0], cotf.at[:, d], s_cx.at[0], dev(dx=d))
     finish_pre(1)
-    hid = [Gather(hidf, s_h, pl.ds(0, 512)), Gather(hidf, s_h2, pl.ds(512, 384))]
+    hid = [Gather(hidf, sems, pl.ds(lo, n)) for sems, lo, n in ((s_h, 0, 512), (s_h2, 512, 256), (s_h3, 768, 128))]
     hid[0].start_z()
     sum_y(3)
     hid[0].start()
     finish_pre(2)
-    finish_pre(3)
-
     hid[1].start_z()
     hid[1].start()
     hid[0].neighbour()
+    finish_pre(3)
+
+    hid[2].start_z()
+    hid[2].start()
     for cp in wdl:
         cp.wait()
     for cp in wdr:
         cp.wait_recv()
+    hid[1].neighbour()
     hid[0].onward(0)
-    hid[1].neighbour()
+    hid[2].neighbour()
     ab = Gather(abf, s_ab, pl.ds(1024, 768))
     ab.start_z()
 
@@ -357,9 +360,12 @@
             hid[0].onward(1)
             hid[1].onward(0)
             hid[1].onward(1)
+            hid[2].onward(0)
+            hid[2].onward(1)
         elif f == 2:
             hid[0].finish()
             hid[1].finish()
+            hid[2].finish()
         return dot(hidf[e].reshape(192, 896), wdf[...])
 
     def after_y():
@@ -671,7 +677,7 @@
         V((4, 2, 96, 1792), BF), V((4, 192, 640), F32),
         V((4, 48, 640), F32), V((4, 3, 48, 640), BF), V((3, 4, 48, 640), BF), V((3, 48, 640), BF), V((3, 48, 640), BF),
         V((640, 896), F32), V((640, 896), BF), V((640, 896), BF), V((4, 160, 896), BF), V((4, 160, 896), BF),
-        D((SLOTS,)), D((4,)), D((5,)), D((3,)), D((1,)), D((4, 2)), D((4,)), D((4,)), D((4,)), D((4,)), D((4,)), D((9,)), D((9,)),
+        D((SLOTS,)), D((4,)), D((5,)), D((3,)), D((1,)), D((4, 2)), D((4,)), D((4,)), D((4,)), D((4,)), D((4,)), D((9,)), D((9,)), D((9,)),
         D((4,)), D((4,)), D((4,)), D((1,)), D((4,)), D((2,)),
         D((3,)), D((4,)), D((1,)), D((1,)), D((9,)),
         D((2,)), D((2,)), D((1,)), D((7,)), D((9,)), D((9,)), D((7,)),

time: 172 us -> 170 us (0.988)
  Pallas kernels: 171 us -> 169 us
where the time goes in v5:
time: 170 us
  Pallas kernels  169 us (99%)
    pallas_call x1, Pallas kernels, body(): pl.pallas_call(kernel, out_shape=shapes, in_specs=[in_any] * 5 + [in_vmem...  167 us

profile of v5, /device:TPU:1, one launch (start us, length us, event | category | flops | bytes accessed | tf_op | source)
XLA Modules:
  0.0 170.2 jit_solution(7034308716385876146)
XLA Ops:
  0.6 167.0 %ffn.1 = (bf16[48,640]{1,0:T(8,128)(2,1)}, bf16[48,640]{1,0:T(8,128)(2,1)}, bf16[160,1728]{1,0:T(8,128)(2,1)}, bf16[160,1728]{1,0:T(8,128)(2,1)}, bf16[432,640]{1,0:T(8,128)(2,1)}) custom-call(bf16[160,1728]{1,0:T(8,128)(2,1)} %gw_ref.1, bf16[160,1728]{1,0:T(8,128)(2,1)} %uw_ref.1, bf16[48,640]{1,0:T(8,128)(2,1)} %tok_ref.1, bf16[432,640]{1,0:T(8,128)(2,1)} %wd_ref.1, ...), custom_call_target="tpu_custom_call" | custom-call | flops 8000000000 | bytes 6000000 | tf_op jit(solution)/shard_map/ffn/pallas_call | solution.py:690
  167.7 2.4 %hand_over.1 = (bf16[48,640]{1,0:T(8,128)(2,1)}, bf16[48,640]{1,0:T(8,128)(2,1)}, bf16[160,1728]{1,0:T(8,128)(2,1)}, bf16[160,1728]{1,0:T(8,128)(2,1)}, bf16[432,640]{1,0:T(8,128)(2,1)}) custom-call(bf16[48,640]{1,0:T(8,128)(2,1)} %get-tuple-element.10.refs_0_, bf16[48,640]{1,0:T(8,128)(2,1)} %get-tuple-element.11.refs_1_, ...), custom_call_target="tpu_custom_call" | custom-call | tf_op jit(solution)/shard_map/hand_over/pallas_call | solution.py:703
